TPU v7x, 128 devices: a whole 4x4x4 slice. The times are simulated.
128 devices in a mesh: frame: 8 (over x_hi, y), pos: 16 (over x_lo, z, core).
Axes of the slice: x: 4 (x_hi: 2, x_lo: 2; x = x_hi * 2 + x_lo), y: 4, z: 4, core: 2. Of those that a mesh axis runs over, the one named last changes fastest.
Arguments:
- inputs: bfloat16 [16, 1536, 1152], P('frame', 'pos'), may hold values from -6 to 6
- cotangent: bfloat16 [16, 1536, 1152], P('frame', 'pos'), may hold values from -6 to 6
- space_projection: bfloat16 [3456, 1152], replicated, may hold values from -2 to 2
- space_output: bfloat16 [1152, 1152], replicated, may hold values from -0.1875 to 0.1875
- time_projection: bfloat16 [3456, 1152], replicated, may hold values from -2 to 2
- time_output: bfloat16 [1152, 1152], replicated, may hold values from -0.1875 to 0.1875
Outputs:
- input_grad: bfloat16 [16, 1536, 1152], P('frame', 'pos')
- space_output_grad: float32 [1152, 1152], P(('frame', 'pos'))
- time_output_grad: float32 [1152, 1152], P(('frame', 'pos'))
All inputs are finite; a program needn't handle non-finite values.
Results may differ from a plain program's by a relative error of at most 0.027.
Values may be sent and summed in bfloat16 or wider, within the bound.
A program may use at most 192 MiB of HBM per device.

v0:
```python
import jax
import jax.numpy as jnp
from jax import lax
from jax.sharding import PartitionSpec as P

HEADS = 16


EPS = 1e-06


def normalize(tokens):
    values = tokens.astype(jnp.float32)
    center = values - jnp.mean(values, axis=-1, keepdims=True)
    inv_std = lax.rsqrt(jnp.mean(center * center, axis=-1, keepdims=True) + EPS)
    return (center * inv_std, inv_std)


def norm_back(grad_hat, normed, inv_std):
    mean_grad = jnp.mean(grad_hat, axis=-1, keepdims=True)
    mean_proj = jnp.mean(grad_hat * normed, axis=-1, keepdims=True)
    return inv_std * (grad_hat - mean_grad - normed * mean_proj)


def project_in(hidden, weight):
    model_width = weight.shape[1]
    weight_three = weight.reshape(3, model_width, model_width)
    result = jnp.einsum("fsi,coi->cfso", hidden, weight_three, preferred_element_type=jnp.float32)
    return result.astype(jnp.bfloat16)


def project_back(gradients, weight):
    model_width = weight.shape[1]
    weight_three = weight.reshape(3, model_width, model_width)
    return jnp.einsum("cfso,coi->fsi", gradients, weight_three, preferred_element_type=jnp.float32)


def layouts(seq_first):
    token_form = "lbhe" if seq_first else "blhe"
    return (token_form, token_form.replace("l", "m"))


def attend(queries, key_vectors, values, seq_first):
    token_form, key_form = layouts(seq_first)
    score_scale = queries.shape[-1] ** (-0.5)
    scores = jnp.einsum(
        token_form + "," + key_form + "->bhlm",
        queries,
        key_vectors,
        preferred_element_type=jnp.float32,
    )
    probability = jax.nn.softmax(scores * score_scale, axis=-1)
    mixed = jnp.einsum(
        "bhlm," + key_form + "->" + token_form,
        probability.astype(jnp.bfloat16),
        values,
        preferred_element_type=jnp.float32,
    )
    return (mixed.astype(jnp.bfloat16), probability)


def attend_back(queries, key_vectors, values, probability, grad_mixed, seq_first):
    token_form, key_form = layouts(seq_first)
    score_scale = queries.shape[-1] ** (-0.5)
    weights = probability.astype(jnp.bfloat16)
    grad_probs = jnp.einsum(
        token_form + "," + key_form + "->bhlm",
        grad_mixed,
        values,
        preferred_element_type=jnp.float32,
    )
    grad_values = jnp.einsum(
        "bhlm," + token_form + "->" + key_form,
        weights,
        grad_mixed,
        preferred_element_type=jnp.float32,
    ).astype(jnp.bfloat16)
    centered = grad_probs - jnp.sum(probability * grad_probs, axis=-1, keepdims=True)
    grad_scores = (probability * centered * score_scale).astype(jnp.bfloat16)
    grad_queries = jnp.einsum(
        "bhlm," + key_form + "->" + token_form,
        grad_scores,
        key_vectors,
        preferred_element_type=jnp.float32,
    ).astype(jnp.bfloat16)
    grad_keys = jnp.einsum(
        "bhlm," + token_form + "->" + key_form,
        grad_scores,
        queries,
        preferred_element_type=jnp.float32,
    ).astype(jnp.bfloat16)
    return jnp.stack([grad_queries, grad_keys, grad_values])


def space_heads(stacked):
    return lax.all_to_all(stacked, "pos", split_axis=3, concat_axis=2, tiled=True)


def space_rows(stacked):
    return lax.all_to_all(stacked, "pos", split_axis=2, concat_axis=3, tiled=True)


def time_heads(stacked):
    return lax.all_to_all(stacked, "frame", split_axis=3, concat_axis=1, tiled=True)


def time_rows(stacked):
    return lax.all_to_all(stacked, "frame", split_axis=1, concat_axis=3, tiled=True)


def shards(inputs, cotangent, space_projection, space_output, time_projection, time_output):
    frames_here, places_here, model_width = inputs.shape
    head_size = model_width // HEADS
    space_hat, space_inv = normalize(inputs)
    space_qkv = project_in(space_hat.astype(jnp.bfloat16), space_projection)
    space_split = space_heads(space_qkv)
    all_places = space_split.shape[2]
    local_heads = space_split.shape[3] // head_size
    space_parts = space_split.reshape(3, frames_here, all_places, local_heads, head_size)
    space_mixed, space_probs = attend(space_parts[0], space_parts[1], space_parts[2], False)
    space_mixed_rows = space_rows(
        space_mixed.reshape(1, frames_here, all_places, local_heads * head_size)
    )[0]
    space_proj = jnp.einsum(
        "fsi,oi->fso", space_mixed_rows, space_output, preferred_element_type=jnp.float32
    )
    stream = (inputs.astype(jnp.float32) + space_proj).astype(jnp.bfloat16)
    time_hat, time_inv = normalize(stream)
    time_qkv = project_in(time_hat.astype(jnp.bfloat16), time_projection)
    time_split = time_heads(time_qkv)
    all_frames = time_split.shape[1]
    time_local = time_split.shape[3] // head_size
    time_parts = time_split.reshape(3, all_frames, places_here, time_local, head_size)
    time_mixed, time_probs = attend(time_parts[0], time_parts[1], time_parts[2], True)
    time_mixed_rows = time_rows(
        time_mixed.reshape(1, all_frames, places_here, time_local * head_size)
    )[0]
    time_grad_part = jnp.einsum(
        "fso,fsi->oi", cotangent, time_mixed_rows, preferred_element_type=jnp.float32
    )
    time_back = jnp.einsum(
        "fso,oi->fsi", cotangent, time_output, preferred_element_type=jnp.float32
    ).astype(jnp.bfloat16)
    time_back_split = time_heads(time_back[None]).reshape(
        all_frames, places_here, time_local, head_size
    )
    time_qkv_grad = attend_back(
        time_parts[0], time_parts[1], time_parts[2], time_probs, time_back_split, True
    )
    time_qkv_rows = time_rows(
        time_qkv_grad.reshape(3, all_frames, places_here, time_local * head_size)
    )
    time_branch = norm_back(project_back(time_qkv_rows, time_projection), time_hat, time_inv)
    upstream = (cotangent.astype(jnp.float32) + time_branch).astype(jnp.bfloat16)
    space_grad_part = jnp.einsum(
        "fso,fsi->oi", upstream, space_mixed_rows, preferred_element_type=jnp.float32
    )
    space_back = jnp.einsum(
        "fso,oi->fsi", upstream, space_output, preferred_element_type=jnp.float32
    ).astype(jnp.bfloat16)
    space_back_split = space_heads(space_back[None]).reshape(
        frames_here, all_places, local_heads, head_size
    )
    space_qkv_grad = attend_back(
        space_parts[0], space_parts[1], space_parts[2], space_probs, space_back_split, False
    )
    space_qkv_rows = space_rows(
        space_qkv_grad.reshape(3, frames_here, all_places, local_heads * head_size)
    )
    space_branch = norm_back(project_back(space_qkv_rows, space_projection), space_hat, space_inv)
    input_grad = (upstream.astype(jnp.float32) + space_branch).astype(jnp.bfloat16)
    space_sum, time_sum = (
        lax.psum_scatter(space_grad_part, ("frame", "pos"), scatter_dimension=0, tiled=True),
        lax.psum_scatter(time_grad_part, ("frame", "pos"), scatter_dimension=0, tiled=True),
    )
    return (input_grad, space_sum, time_sum)


def solution(mesh):
    return jax.shard_map(
        shards,
        mesh=mesh,
        in_specs=(P("frame", "pos", None), P("frame", "pos", None), P(), P(), P(), P()),
        out_specs=(P("frame", "pos", None), P(("frame", "pos"), None), P(("frame", "pos"), None)),
        check_vma=False,
    )
```

profile of v0, /device:TPU:1, one launch (start us, length us, event | category | flops | bytes accessed | tf_op | source)
XLA Modules:
  0.0 448.2 jit_solution(15719015555821328096)
XLA Ops:
  7.2 1.3 convert_reduce_fusion
  8.5 1.3 fusion.91
  10.4 7.1 %fusion.19 = bf16[3,2,96,1152]{3,2,0,1:T(8,128)(2,1)} fusion(bf16[3,1152,1152,1]{2,1,0,3:T(8,128)(2,1)} %bitcast.186, bf16[2,96,1152]{2,1,0:T(8,128)(2,1)} %param.6, f32[2,96]{1,0:T(2,128)S(1)} %add_rsqrt_fusion.1, f32[2,96]{1,0:T(2,128)S(1)} %broadcast_multiply_fusion.5), kind=kOutput, calls=%fused_computation.22 | convolution fusion | flops 1530372096 | bytes 9733632 | tf_op jit(solution)/shard_map/fsi,coi->cfso/dot_general | solution.py:28
  17.5 5.1 %copy.111 = bf16[3,2,96,1152]{2,1,0,3:T(2,128)(2,1)} copy(bf16[3,2,96,1152]{3,2,0,1:T(8,128)(2,1)} %fusion.19) | data formatting | bytes 2654208 | tf_op jit(solution)/shard_map/convert_element_type | solution.py:29
  22.6 31.3 %all_to_all.126 = bf16[3,2,96,1152]{2,1,0,3:T(2,128)(2,1)S(1)} all-to-all(bf16[3,2,96,1152]{2,1,0,3:T(2,128)(2,1)} %copy.111), channel_id=1, replica_groups=mesh['frame'=8,'pos'=16] {'pos'}, dimensions={3} | all-to-all | bytes 2654208 | tf_op jit(solution)/shard_map/all_to_all | solution.py:96
  56.0 2.4 reshape.166
  58.4 2.0 copy.115
  60.4 2.5 reshape.167
  63.7 1.7 reshape.165
  65.4 11.3 %fusion.130 = (f32[2,1536]{1,0:T(2,128)S(1)}, f32[2,1536,1536]{1,2,0:T(8,128)}) fusion(bf16[2,1536,72]{1,2,0:T(8,128)(2,1)} %reshape.166, bf16[2,1536,72]{1,2,0:T(8,128)(2,1)} %reshape.167), kind=kOutput, calls=%fused_computation.117 | convolution fusion | flops 693634560 | bytes 19771392 | tf_op jit(solution)/shard_map/sub | solution.py:52
  76.7 9.6 %fusion.65 = bf16[1,2,1536,72]{2,3,1,0:T(8,128)(2,1)S(1)} fusion(bf16[2,1536,72]{1,2,0:T(8,128)(2,1)S(1)} %reshape.165, f32[2,1536]{1,0:T(2,128)S(1)} %get-tuple-element.27, bf16[2,1536,72]{1,2,0:T(8,128)(2,1)} %reshape.166, bf16[2,1536,72]{1,2,0:T(8,128)(2,1)} %reshape.167), kind=kOutput, calls=%fused_computation.45 | convolution fusion | flops 1378054656 | bytes 1781760 | tf_op jit(solution)/shard_map/bhlm,bmhe->blhe/dot_general | solution.py:53
  86.3 1.8 copy.117
  88.1 4.8 %all-to-all-start.1 = ((bf16[1,2,1536,72]{3,1,0,2:T(2,128)(2,1)}), bf16[1,2,1536,72]{3,1,0,2:T(2,128)(2,1)}, u32[]{:S(2)}, u32[]{:S(2)}) async-start(bf16[1,2,1536,72]{3,1,0,2:T(2,128)(2,1)} %copy.117), calls=%async_computation.1 | async-start | bytes 1572864 | tf_op jit(solution)/shard_map/all_to_all | solution.py:100
  93.0 2.5 fusion.50
  95.5 1.3 copy.126
  96.8 9.3 %all-to-all-done.1 = bf16[1,2,1536,72]{3,1,0,2:T(2,128)(2,1)} async-done(((bf16[1,2,1536,72]{3,1,0,2:T(2,128)(2,1)}), bf16[1,2,1536,72]{3,1,0,2:T(2,128)(2,1)}, u32[]{:S(2)}, u32[]{:S(2)}) %all-to-all-start.1) | async-done | bytes 442400 | tf_op jit(solution)/shard_map/all_to_all | solution.py:100
  106.1 6.4 %all-to-all-start.3 = ((bf16[1,2,96,1152]{2,1,0,3:T(2,128)(2,1)}), bf16[1,2,96,1152]{2,1,0,3:T(2,128)(2,1)}, u32[]{:S(2)}, u32[]{:S(2)}) async-start(bf16[1,2,96,1152]{2,1,0,3:T(2,128)(2,1)} %copy.126), calls=%async_computation.3 | async-start | bytes 1179648 | tf_op jit(solution)/shard_map/all_to_all | solution.py:104
  112.5 3.0 copy.118
  115.5 2.3 fusion.131
  118.1 7.0 %fusion.20 = bf16[3,2,96,1152]{3,2,0,1:T(8,128)(2,1)} fusion(bf16[3,1152,1152,1]{2,1,0,3:T(8,128)(2,1)} %bitcast.184, f32[2,96,1152]{2,1,0:T(8,128)S(1)} %get-tuple-element.30, f32[2,96]{1,0:T(2,128)S(1)} %add_rsqrt_fusion, f32[2,96]{1,0:T(2,128)S(1)} %broadcast_multiply_fusion.4), kind=kOutput, calls=%fused_computation.23 | convolution fusion | flops 1530150912 | bytes 10176000 | tf_op jit(solution)/shard_map/fsi,coi->cfso/dot_general | solution.py:28
  125.0 5.1 %copy.120 = bf16[3,2,96,1152]{2,1,0,3:T(2,128)(2,1)} copy(bf16[3,2,96,1152]{3,2,0,1:T(8,128)(2,1)} %fusion.20) | data formatting | bytes 2654208 | tf_op jit(solution)/shard_map/convert_element_type | solution.py:29
  130.2 7.1 %all-to-all-start.2 = ((bf16[3,2,96,1152]{2,1,0,3:T(2,128)(2,1)}), bf16[3,2,96,1152]{2,1,0,3:T(2,128)(2,1)}, u32[]{:S(2)}, u32[]{:S(2)}) async-start(bf16[3,2,96,1152]{2,1,0,3:T(2,128)(2,1)} %copy.120), calls=%async_computation.2 | async-start | bytes 3538944 | tf_op jit(solution)/shard_map/all_to_all | solution.py:104
  139.3 3.0 copy.130
  142.3 17.4 %all-to-all-done.2 = bf16[3,2,96,1152]{2,1,0,3:T(2,128)(2,1)} async-done(((bf16[3,2,96,1152]{2,1,0,3:T(2,128)(2,1)}), bf16[3,2,96,1152]{2,1,0,3:T(2,128)(2,1)}, u32[]{:S(2)}, u32[]{:S(2)}) %all-to-all-start.2) | async-done | bytes 1327136 | tf_op jit(solution)/shard_map/all_to_all | solution.py:104
  159.6 1.7 copy.121
  163.4 3.0 copy.124
  166.4 2.0 copy.122
  168.3 3.0 copy.132
  171.3 2.0 copy.129
  173.3 3.1 copy.131
  176.4 4.1 fusion.132
  180.4 3.2 fusion.133
  183.7 1.4 fusion.76
  185.1 4.9 %fusion.73 = bf16[16,96,2,72]{3,0,2,1:T(8,128)(2,1)} fusion(bf16[16,96,2,72]{3,0,2,1:T(8,128)(2,1)} %copy.132, f32[96,2,16,16]{2,3,1,0:T(8,128)} %fusion.133, f32[96,2,16,16]{2,3,1,0:T(8,128)} %get-tuple-element.32, f32[96,2,16]{2,1,0:T(2,128)} %get-tuple-element.31), kind=kOutput, calls=%fused_computation.60 | convolution fusion | flops 7646223 | bytes 1290240 | tf_op jit(solution)/shard_map/bhlm,mbhe->lbhe/dot_general | solution.py:80
  190.0 4.8 %fusion.74 = bf16[16,96,2,72]{3,0,2,1:T(8,128)(2,1)} fusion(bf16[16,96,2,72]{3,0,2,1:T(8,128)(2,1)} %copy.124, f32[96,2,16,16]{2,3,1,0:T(8,128)} %fusion.133, f32[96,2,16,16]{2,3,1,0:T(8,128)} %get-tuple-element.32, f32[96,2,16]{2,1,0:T(2,128)} %get-tuple-element.31), kind=kOutput, calls=%fused_computation.61 | convolution fusion | flops 7646223 | bytes 1290240 | tf_op jit(solution)/shard_map/bhlm,lbhe->mbhe/dot_general | solution.py:86
  194.8 2.7 copy.155
  197.5 5.5 %all-to-all-start.7 = ((bf16[1,16,96,144]{2,3,0,1:T(8,128)(2,1)}), bf16[1,16,96,144]{2,3,0,1:T(8,128)(2,1)}, u32[]{:S(2)}, u32[]{:S(2)}) async-start(bf16[1,16,96,144]{2,3,0,1:T(8,128)(2,1)} %bitcast.200), calls=%async_computation.7 | async-start | bytes 1179648 | tf_op jit(solution)/shard_map/all_to_all | solution.py:108
  203.0 2.7 copy.134
  205.7 2.7 copy.136
  208.4 2.8 fusion.75
  211.2 2.7 copy.138
  213.9 1.8 pad_maximum_fusion
  215.8 1.3 copy.139
  217.1 6.6 %all-to-all-start.4 = ((bf16[3,16,96,144]{2,3,0,1:T(8,128)(2,1)}), bf16[3,16,96,144]{2,3,0,1:T(8,128)(2,1)}, u32[]{:S(2)}, u32[]{:S(2)}) async-start(bf16[3,16,96,144]{2,3,0,1:T(8,128)(2,1)} %copy.139), calls=%async_computation.4 | async-start | bytes 3538944 | tf_op jit(solution)/shard_map/all_to_all | solution.py:108
  224.9 4.3 convolution_bitcast_fusion
  229.2 17.2 %all-to-all-done.4 = bf16[3,16,96,144]{2,3,0,1:T(8,128)(2,1)} async-done(((bf16[3,16,96,144]{2,3,0,1:T(8,128)(2,1)}), bf16[3,16,96,144]{2,3,0,1:T(8,128)(2,1)}, u32[]{:S(2)}, u32[]{:S(2)}) %all-to-all-start.4) | async-done | bytes 1327136 | tf_op jit(solution)/shard_map/all_to_all | solution.py:108
  246.5 1.6 copy.141
  248.1 5.5 %fusion.127 = (f32[2,96]{1,0:T(2,128)S(1)}, f32[2,96]{1,0:T(2,128)S(1)}, f32[2,96,1152]{2,1,0:T(8,128)S(1)}) fusion(f32[2,96]{1,0:T(2,128)S(1)} %add_rsqrt_fusion, f32[2,96,1152]{2,1,0:T(8,128)S(1)} %get-tuple-element.30, f32[2,96]{1,0:T(2,128)S(1)} %broadcast_multiply_fusion.4, bf16[3,2,96,1152]{2,3,1,0:T(8,128)(2,1)S(1)} %bitcast.191, ...), kind=kOutput, calls=%fused_computation.114 | convolution fusion | flops 1529929216 | bytes 11062272 | tf_op jit(solution)/shard_map/cfso,coi->fsi/dot_general | solution.py:35
  254.8 3.3 convolution_bitcast_fusion.1
  260.7 18.3 %all_to_all.127 = bf16[1,2,96,1152]{2,1,0,3:T(2,128)(2,1)S(1)} all-to-all(bf16[1,2,96,1152]{2,1,0,3:T(2,128)(2,1)S(1)} %copy.143), channel_id=1, replica_groups=mesh['frame'=8,'pos'=16] {'pos'}, dimensions={3} | all-to-all | bytes 884736 | tf_op jit(solution)/shard_map/all_to_all | solution.py:96
  279.8 8.2 %fusion.134 = f32[2,1536,1536]{1,2,0:T(8,128)} fusion(bf16[2,1536,72]{1,2,0:T(8,128)(2,1)S(1)} %reshape.171, bf16[2,1536,72]{1,2,0:T(8,128)(2,1)S(1)} %copy-done.10), kind=kOutput, calls=%fused_computation.121 | convolution fusion | flops 679477248 | bytes 19759104 | tf_op jit(solution)/shard_map/blhe,bmhe->bhlm/dot_general | solution.py:66
  288.0 27.0 %fusion.59 = bf16[1,2,1536,1,72]{2,4,1,3,0:T(8,128)(2,1)S(1)} fusion(bf16[2,1536,72]{1,2,0:T(8,128)(2,1)S(1)} %copy-done.12, f32[2,1536,1536]{1,2,0:T(8,128)} %fusion.134, f32[2,1536,1536]{1,2,0:T(8,128)} %get-tuple-element.28, f32[2,1536]{1,0:T(2,128)S(1)} %copy-done.20), kind=kOutput, calls=%fused_computation.43 | convolution fusion | flops 712733184 | bytes 38645760 | tf_op jit(solution)/shard_map/bhlm,bmhe->blhe/dot_general | solution.py:80
  315.0 25.8 %fusion.56 = bf16[1,2,1536,1,72]{2,4,1,3,0:T(8,128)(2,1)S(1)} fusion(bf16[2,1536,72]{1,2,0:T(8,128)(2,1)S(1)} %copy-done.11, f32[2,1536,1536]{1,2,0:T(8,128)} %fusion.134, f32[2,1536,1536]{1,2,0:T(8,128)} %get-tuple-element.28, f32[2,1536]{1,0:T(2,128)S(1)} %copy-done.20), kind=kOutput, calls=%fused_computation.42 | convolution fusion | flops 712733184 | bytes 38645760 | tf_op jit(solution)/shard_map/bhlm,blhe->bmhe/dot_general | solution.py:86
  340.8 8.8 %fusion.62 = bf16[1,2,1536,1,72]{2,4,1,3,0:T(8,128)(2,1)} fusion(bf16[2,1536,72]{1,2,0:T(8,128)(2,1)S(1)} %reshape.171, f32[2,1536]{1,0:T(2,128)S(1)} %copy-done.20, bf16[2,1536,72]{1,2,0:T(8,128)(2,1)S(1)} %copy-done.11, bf16[2,1536,72]{1,2,0:T(8,128)(2,1)S(1)} %copy-done.12), kind=kOutput, calls=%fused_computation.44 | convolution fusion | flops 1378054656 | bytes 1781760 | tf_op jit(solution)/shard_map/bhlm,blhe->bmhe/dot_general | solution.py:72
  349.6 1.2 maximum_bitcast_fusion
  350.7 4.5 %copy.149 = bf16[3,2,1536,72]{3,1,0,2:T(2,128)(2,1)} copy(bf16[3,2,1536,72]{2,3,1,0:T(8,128)(2,1)S(1)} %maximum_bitcast_fusion) | data formatting | bytes 2654208 | tf_op jit(solution)/shard_map/reshape | solution.py:168
  355.3 4.2 all-to-all-start.6
  359.5 33.6 %all-to-all-done.6 = bf16[3,2,1536,72]{3,1,0,2:T(2,128)(2,1)S(1)} async-done(((bf16[3,2,1536,72]{3,1,0,2:T(2,128)(2,1)}), bf16[3,2,1536,72]{3,1,0,2:T(2,128)(2,1)S(1)}, u32[]{:S(2)}, u32[]{:S(2)}) %all-to-all-start.6) | async-done | bytes 1327136 | tf_op jit(solution)/shard_map/all_to_all | solution.py:100
  393.1 3.9 copy.150
  397.0 6.1 %fusion.126 = (f32[2,96]{1,0:T(2,128)S(1)}, f32[2,96]{1,0:T(2,128)S(1)}, f32[2,96,1152]{2,1,0:T(8,128)S(1)}) fusion(f32[2,96]{1,0:T(2,128)S(1)} %copy-done.16, f32[2,96]{1,0:T(2,128)S(1)} %copy-done.14, bf16[2,96,1152]{2,1,0:T(8,128)(2,1)S(1)} %copy-done.2, bf16[3,2,96,1152]{2,3,1,0:T(8,128)(2,1)} %bitcast.190, bf16[3,1152,1152,1]{2,1,3,0:T(8,128)(2,1)} %bitcast.187), kind=kOutput, calls=%fused_computation.113 | convolution fusion | flops 1530150400 | bytes 10619904 | tf_op jit(solution)/shard_map/cfso,coi->fsi/dot_general | solution.py:35
  403.1 1.2 fusion.90
  404.3 33.0 %all-reduce.5.cloned.1.call-done = (f32[1152,1152]{1,0:T(8,128)}, f32[1152,1152]{0,1:T(8,128)}) async-done(((f32[1152,1152]{1,0:T(8,128)}, f32[1152,1152]{0,1:T(8,128)}), (f32[1152,1152]{1,0:T(8,128)}, f32[1152,1152]{0,1:T(8,128)})) %all-reduce.5.cloned.1.call-update) | async-done | bytes 10616848
  437.2 1.5 constant_dynamic-slice_fusion
  439.6 1.5 constant_dynamic-slice_fusion.1
  (70 shorter events, 14.3 us)
Async XLA Ops:
  7.2 108.3 %copy-start = (bf16[1152,1152]{1,0:T(8,128)(2,1)S(1)}, bf16[1152,1152]{1,0:T(8,128)(2,1)}, u32[]{:S(2)}) copy-start(bf16[1152,1152]{1,0:T(8,128)(2,1)} %param.9) | copy-start | bytes 7962628
  8.5 1.3 copy-start.13
  9.8 0.6 copy-start.15
  65.4 11.3 %copy-start.9 = (bf16[2,1536,72]{1,2,0:T(8,128)(2,1)}, bf16[2,1536,72]{1,2,0:T(8,128)(2,1)S(1)}, u32[]{:S(2)}) copy-start(bf16[2,1536,72]{1,2,0:T(8,128)(2,1)S(1)} %reshape.165) | copy-start | bytes 1327108
  76.7 9.6 %copy-start.19 = (f32[2,1536]{1,0:T(2,128)}, f32[2,1536]{1,0:T(2,128)S(1)}, u32[]{:S(2)}) copy-start(f32[2,1536]{1,0:T(2,128)S(1)} %get-tuple-element.27) | copy-start | bytes 36868
  86.3 6.6 %copy-start.6 = (bf16[2,96,1152]{2,1,0:T(8,128)(2,1)S(1)}, bf16[2,96,1152]{2,1,0:T(8,128)(2,1)}, u32[]{:S(2)}) copy-start(bf16[2,96,1152]{2,1,0:T(8,128)(2,1)} %param.7) | copy-start | bytes 1327108
  88.1 18.0 %all-to-all-start.1 = ((bf16[1,2,1536,72]{3,1,0,2:T(2,128)(2,1)}), bf16[1,2,1536,72]{3,1,0,2:T(2,128)(2,1)}, u32[]{:S(2)}, u32[]{:S(2)}) async-start(bf16[1,2,1536,72]{3,1,0,2:T(2,128)(2,1)} %copy.117), calls=%async_computation.1 | async-start | bytes 1572864 | tf_op jit(solution)/shard_map/all_to_all | solution.py:100
  106.1 24.0 %all-to-all-start.3 = ((bf16[1,2,96,1152]{2,1,0,3:T(2,128)(2,1)}), bf16[1,2,96,1152]{2,1,0,3:T(2,128)(2,1)}, u32[]{:S(2)}, u32[]{:S(2)}) async-start(bf16[1,2,96,1152]{2,1,0,3:T(2,128)(2,1)} %copy.126), calls=%async_computation.3 | async-start | bytes 1179648 | tf_op jit(solution)/shard_map/all_to_all | solution.py:104
  130.2 29.5 %all-to-all-start.2 = ((bf16[3,2,96,1152]{2,1,0,3:T(2,128)(2,1)}), bf16[3,2,96,1152]{2,1,0,3:T(2,128)(2,1)}, u32[]{:S(2)}, u32[]{:S(2)}) async-start(bf16[3,2,96,1152]{2,1,0,3:T(2,128)(2,1)} %copy.120), calls=%async_computation.2 | async-start | bytes 3538944 | tf_op jit(solution)/shard_map/all_to_all | solution.py:104
  180.4 3.2 copy-start.8
  180.4 3.2 copy-start.17
  180.4 3.2 copy-start.18
  197.5 19.6 %all-to-all-start.7 = ((bf16[1,16,96,144]{2,3,0,1:T(8,128)(2,1)}), bf16[1,16,96,144]{2,3,0,1:T(8,128)(2,1)}, u32[]{:S(2)}, u32[]{:S(2)}) async-start(bf16[1,16,96,144]{2,3,0,1:T(8,128)(2,1)} %bitcast.200), calls=%async_computation.7 | async-start | bytes 1179648 | tf_op jit(solution)/shard_map/all_to_all | solution.py:108
  217.1 29.3 %all-to-all-start.4 = ((bf16[3,16,96,144]{2,3,0,1:T(8,128)(2,1)}), bf16[3,16,96,144]{2,3,0,1:T(8,128)(2,1)}, u32[]{:S(2)}, u32[]{:S(2)}) async-start(bf16[3,16,96,144]{2,3,0,1:T(8,128)(2,1)} %copy.139), calls=%async_computation.4 | async-start | bytes 3538944 | tf_op jit(solution)/shard_map/all_to_all | solution.py:108
  223.8 213.4 %all-reduce.5.cloned.1.call-start = ((), (), s32[]{:S(2)}) async-start(), calls=%async_computation.8 | async-start | bytes 21233664
  248.1 5.6 %copy-start.7 = (bf16[2,96,1152]{2,1,0:T(8,128)(2,1)S(1)}, bf16[2,96,1152]{2,1,0:T(8,128)(2,1)}, u32[]{:S(2)}) copy-start(bf16[2,96,1152]{2,1,0:T(8,128)(2,1)} %param.7) | copy-start | bytes 1327108
  253.6 1.2 copy-start.5
  254.0 0.8 copy-start.3
  258.1 1.0 copy-start.4
  259.9 19.8 %copy-start.10 = (bf16[2,1536,72]{1,2,0:T(8,128)(2,1)S(1)}, bf16[2,1536,72]{1,2,0:T(8,128)(2,1)}, u32[]{:S(2)}) copy-start(bf16[2,1536,72]{1,2,0:T(8,128)(2,1)} %copy-done.9) | copy-start | bytes 1327108
  279.7 8.2 %copy-start.12 = (bf16[2,1536,72]{1,2,0:T(8,128)(2,1)S(1)}, bf16[2,1536,72]{1,2,0:T(8,128)(2,1)}, u32[]{:S(2)}) copy-start(bf16[2,1536,72]{1,2,0:T(8,128)(2,1)} %reshape.167) | copy-start | bytes 1327108
  279.7 8.2 %copy-start.20 = (f32[2,1536]{1,0:T(2,128)S(1)}, f32[2,1536]{1,0:T(2,128)}, u32[]{:S(2)}) copy-start(f32[2,1536]{1,0:T(2,128)} %copy-done.19) | copy-start | bytes 36868
  288.0 27.0 %copy-start.11 = (bf16[2,1536,72]{1,2,0:T(8,128)(2,1)S(1)}, bf16[2,1536,72]{1,2,0:T(8,128)(2,1)}, u32[]{:S(2)}) copy-start(bf16[2,1536,72]{1,2,0:T(8,128)(2,1)} %reshape.166) | copy-start | bytes 1327108
  355.3 37.8 %all-to-all-start.6 = ((bf16[3,2,1536,72]{3,1,0,2:T(2,128)(2,1)}), bf16[3,2,1536,72]{3,1,0,2:T(2,128)(2,1)S(1)}, u32[]{:S(2)}, u32[]{:S(2)}) async-start(bf16[3,2,1536,72]{3,1,0,2:T(2,128)(2,1)} %copy.149), calls=%async_computation.6 | async-start | bytes 4718592 | tf_op jit(solution)/shard_map/all_to_all | solution.py:100
  359.5 37.5 %copy-start.2 = (bf16[2,96,1152]{2,1,0:T(8,128)(2,1)S(1)}, bf16[2,96,1152]{2,1,0:T(8,128)(2,1)}, u32[]{:S(2)}) copy-start(bf16[2,96,1152]{2,1,0:T(8,128)(2,1)} %param.6) | copy-start | bytes 1327108
  359.5 37.5 %copy-start.14 = (f32[2,96]{1,0:T(2,128)S(1)}, f32[2,96]{1,0:T(2,128)}, u32[]{:S(2)}) copy-start(f32[2,96]{1,0:T(2,128)} %copy-done.13) | copy-start | bytes 2308
  359.5 37.5 %copy-start.16 = (f32[2,96]{1,0:T(2,128)S(1)}, f32[2,96]{1,0:T(2,128)}, u32[]{:S(2)}) copy-start(f32[2,96]{1,0:T(2,128)} %copy-done.15) | copy-start | bytes 2308
  396.9 44.2 %copy-start.1 = (bf16[1152,1152]{1,0:T(8,128)(2,1)S(1)}, bf16[1152,1152]{1,0:T(8,128)(2,1)}, u32[]{:S(2)}) copy-start(bf16[1152,1152]{1,0:T(8,128)(2,1)} %param.9) | copy-start | bytes 7962628
Sparse Core Ops, SparseCore 0:
  258.3 178.9 all-reduce.4
where the time goes:
time: 456 us; the launch traced here: 448 us
  matrix products  151 us (33%)
  waiting for transfers between devices  111 us (24%)
  local copies, waits for them, and re-layouts  80.4 us (18%)
  blocking collectives  49.5 us (11%)
  starting transfers between devices  34.7 us (8%)
  between operations  14.6 us (3%)
  other arithmetic  7.4 us (2%)
    all_to_all x2, blocking collectives, space_heads(): lax.all_to_all(stacked, 'pos', split_axis=3, concat_axis=2, tiled=True)  49.5 us
    all_to_all x2, waiting for transfers between devices, space_rows(): lax.all_to_all(stacked, 'pos', split_axis=2, concat_axis=3, tiled=True)  42.9 us
    unnamed x2, waiting for transfers between devices  33 us
    dot_general x2, matrix products, attend_back(): jnp.einsum('bhlm,' + key_form + '->' + token_form, grad_scores, key_vecto...  31.9 us
    dot_general x2, matrix products, attend_back(): jnp.einsum('bhlm,' + token_form + '->' + key_form, grad_scores, queries,...  30.6 us
    all_to_all x2, waiting for transfers between devices, time_heads(): lax.all_to_all(stacked, 'frame', split_axis=3, concat_axis=1, tiled=True)  17.4 us
    all_to_all x2, waiting for transfers between devices, time_rows(): lax.all_to_all(stacked, 'frame', split_axis=1, concat_axis=3, tiled=True)  17.2 us
    sub x2, matrix products, attend(): probability = jax.nn.softmax(scores * score_scale, axis=-1)  15.4 us
  transfers between devices with their start and end apart: 7, of which 5 were waited for; matrix products, arithmetic and copies ran while one was open for 30% of the time, Pallas kernels for 0%

commit v1 on v0

--- a/solution.py
+++ b/solution.py
@@ -100,17 +100,32 @@
     return lax.all_to_all(stacked, "pos", split_axis=2, concat_axis=3, tiled=True)
 
 
-def time_heads(stacked):
-    return lax.all_to_all(stacked, "frame", split_axis=3, concat_axis=1, tiled=True)
-
-
-def time_rows(stacked):
-    return lax.all_to_all(stacked, "frame", split_axis=1, concat_axis=3, tiled=True)
+def to_time(rows):
+    return lax.all_to_all(rows, "frame", split_axis=1, concat_axis=0, tiled=True)
+
+
+def to_rows(tokens):
+    return lax.all_to_all(tokens, "frame", split_axis=0, concat_axis=1, tiled=True)
+
+
+def time_mask(frames, places):
+    place = jnp.arange(frames * places) % places
+    return place[:, None] == place[None, :]
+
+
+def scatter_sum(partial):
+    devices = lax.axis_size("frame") * lax.axis_size("pos")
+    rows, width = partial.shape
+    flat = partial.reshape(devices, rows * width // devices // 128, 128)
+    out = lax.psum_scatter(flat, ("frame", "pos"), scatter_dimension=0, tiled=False)
+    return out.reshape(rows // devices, width)
 
 
 def shards(inputs, cotangent, space_projection, space_output, time_projection, time_output):
     frames_here, places_here, model_width = inputs.shape
     head_size = model_width // HEADS
+    scale = head_size ** (-0.5)
+    cot_time = to_time(cotangent)
     space_hat, space_inv = normalize(inputs)
     space_qkv = project_in(space_hat.astype(jnp.bfloat16), space_projection)
     space_split = space_heads(space_qkv)
@@ -124,37 +139,50 @@
     space_proj = jnp.einsum(
         "fsi,oi->fso", space_mixed_rows, space_output, preferred_element_type=jnp.float32
     )
-    stream = (inputs.astype(jnp.float32) + space_proj).astype(jnp.bfloat16)
-    time_hat, time_inv = normalize(stream)
-    time_qkv = project_in(time_hat.astype(jnp.bfloat16), time_projection)
-    time_split = time_heads(time_qkv)
-    all_frames = time_split.shape[1]
-    time_local = time_split.shape[3] // head_size
-    time_parts = time_split.reshape(3, all_frames, places_here, time_local, head_size)
-    time_mixed, time_probs = attend(time_parts[0], time_parts[1], time_parts[2], True)
-    time_mixed_rows = time_rows(
-        time_mixed.reshape(1, all_frames, places_here, time_local * head_size)
-    )[0]
-    time_grad_part = jnp.einsum(
-        "fso,fsi->oi", cotangent, time_mixed_rows, preferred_element_type=jnp.float32
-    )
-    time_back = jnp.einsum(
-        "fso,oi->fsi", cotangent, time_output, preferred_element_type=jnp.float32
-    ).astype(jnp.bfloat16)
-    time_back_split = time_heads(time_back[None]).reshape(
-        all_frames, places_here, time_local, head_size
-    )
-    time_qkv_grad = attend_back(
-        time_parts[0], time_parts[1], time_parts[2], time_probs, time_back_split, True
-    )
-    time_qkv_rows = time_rows(
-        time_qkv_grad.reshape(3, all_frames, places_here, time_local * head_size)
-    )
-    time_branch = norm_back(project_back(time_qkv_rows, time_projection), time_hat, time_inv)
-    upstream = (cotangent.astype(jnp.float32) + time_branch).astype(jnp.bfloat16)
+    stream_rows = (inputs.astype(jnp.float32) + space_proj).astype(jnp.bfloat16)
+    stream = to_time(stream_rows)
+    frames, places, _ = stream.shape
+    tokens = frames * places
+    time_hat, time_inv = normalize(stream.reshape(tokens, model_width))
+    qkv = jnp.einsum(
+        "ti,oi->to",
+        time_hat.astype(jnp.bfloat16),
+        time_projection,
+        preferred_element_type=jnp.float32,
+    ).astype(jnp.bfloat16)
+    q, k, v = (
+        qkv[:, c * model_width : (c + 1) * model_width].reshape(tokens, HEADS, head_size)
+        for c in range(3)
+    )
+    mask = time_mask(frames, places)
+    scores = jnp.einsum("the,she->hts", q, k, preferred_element_type=jnp.float32) * scale
+    probs = jax.nn.softmax(jnp.where(mask, scores, -jnp.inf), axis=-1)
+    weights = probs.astype(jnp.bfloat16)
+    time_mixed = jnp.einsum("hts,she->the", weights, v, preferred_element_type=jnp.float32)
+    time_mixed = time_mixed.astype(jnp.bfloat16).reshape(tokens, model_width)
+    cot = cot_time.reshape(tokens, model_width)
+    time_grad_part = jnp.einsum("to,ti->oi", cot, time_mixed, preferred_element_type=jnp.float32)
+    time_sum = scatter_sum(time_grad_part)
+    back = jnp.einsum("to,oi->ti", cot, time_output, preferred_element_type=jnp.float32)
+    back = back.astype(jnp.bfloat16).reshape(tokens, HEADS, head_size)
+    grad_probs = jnp.einsum("the,she->hts", back, v, preferred_element_type=jnp.float32)
+    grad_v = jnp.einsum("hts,the->she", weights, back, preferred_element_type=jnp.float32)
+    centered = grad_probs - jnp.sum(probs * grad_probs, axis=-1, keepdims=True)
+    grad_scores = (probs * centered * scale).astype(jnp.bfloat16)
+    grad_q = jnp.einsum("hts,she->the", grad_scores, k, preferred_element_type=jnp.float32)
+    grad_k = jnp.einsum("hts,the->she", grad_scores, q, preferred_element_type=jnp.float32)
+    grads = jnp.concatenate(
+        [g.astype(jnp.bfloat16).reshape(tokens, model_width) for g in (grad_q, grad_k, grad_v)],
+        axis=1,
+    )
+    grad_hat = jnp.einsum("to,oi->ti", grads, time_projection, preferred_element_type=jnp.float32)
+    upstream_time = cot.astype(jnp.float32) + norm_back(grad_hat, time_hat, time_inv)
+    upstream_time = upstream_time.astype(jnp.bfloat16)
+    upstream = to_rows(upstream_time.reshape(frames, places, model_width))
     space_grad_part = jnp.einsum(
         "fso,fsi->oi", upstream, space_mixed_rows, preferred_element_type=jnp.float32
     )
+    space_sum = scatter_sum(space_grad_part)
     space_back = jnp.einsum(
         "fso,oi->fsi", upstream, space_output, preferred_element_type=jnp.float32
     ).astype(jnp.bfloat16)
@@ -169,10 +197,6 @@
     )
     space_branch = norm_back(project_back(space_qkv_rows, space_projection), space_hat, space_inv)
     input_grad = (upstream.astype(jnp.float32) + space_branch).astype(jnp.bfloat16)
-    space_sum, time_sum = (
-        lax.psum_scatter(space_grad_part, ("frame", "pos"), scatter_dimension=0, tiled=True),
-        lax.psum_scatter(time_grad_part, ("frame", "pos"), scatter_dimension=0, tiled=True),
-    )
     return (input_grad, space_sum, time_sum)
 
 

time: 456 us -> 1490 us (3.27)
  waiting for transfers between devices: 111 us -> 1090 us
  blocking collectives: 49.5 us -> 99.9 us
  starting transfers between devices: 34.7 us -> 16.6 us
    unnamed x2 -> x4, waiting for transfers between devices: 33 us -> 1080 us
    all_to_all x0 -> x2, blocking collectives: none -> 49.6 us  [the longest x1 34.7 us: space_rows(): lax.all_to_all(stacked, 'pos', split_axis=2, concat_axis=3, tiled=True)]
    dot_general x2 -> x9, matrix products: 6.85 us -> 40.9 us  [the longest x1 6.99 us: shards(): jnp.einsum('hts,she->the', grad_scores, k, preferred_element_type=jnp.flo...]
    all_to_all x2 -> x1, waiting for transfers between devices: 42.9 us -> 12.1 us  [space_rows(): lax.all_to_all(stacked, 'pos', split_axis=2, concat_axis=3, tiled=True)]
    all_to_all x4 -> x2, waiting for transfers between devices: 34.6 us -> 5.75 us  [to_time(): lax.all_to_all(rows, 'frame', split_axis=1, concat_axis=0, tiled=True)]
    dot_general x2 -> x1, matrix products: 31.9 us -> 25.2 us  [attend_back(): jnp.einsum('bhlm,' + key_form + '->' + token_form, grad_scores, key_vecto...]
    dot_general x2 -> x1, matrix products: 30.6 us -> 25.7 us  [attend_back(): jnp.einsum('bhlm,' + token_form + '->' + key_form, grad_scores, queries,...]
  transfers between devices with their start and end apart: 7 -> 5, of which waited for: 5 -> 5; matrix products, arithmetic and copies ran while one was open for 30% -> 10% of each run, Pallas kernels for 0% -> 0%
where the time goes in v1:
time: 1490 us; the launch traced here: 1480 us
  waiting for transfers between devices  1090 us (73%)
  matrix products  156 us (10%)
  blocking collectives  99.9 us (7%)
  local copies, waits for them, and re-layouts  83.9 us (6%)
  starting transfers between devices  16.6 us (1%)
    unnamed x4, waiting for transfers between devices  1080 us
    all_to_all x2, blocking collectives, space_heads(): lax.all_to_all(stacked, 'pos', split_axis=3, concat_axis=2, tiled=True)  50.3 us
    all_to_all x1, blocking collectives, space_rows(): lax.all_to_all(stacked, 'pos', split_axis=2, concat_axis=3, tiled=True)  34.7 us
  transfers between devices with their start and end apart: 5, of which 5 were waited for; matrix products, arithmetic and copies ran while one was open for 10% of the time, Pallas kernels for 0%

profile of v1, /device:TPU:1, one launch (start us, length us, event | category | flops | bytes accessed | tf_op | source)
XLA Modules:
  0.0 1477.4 jit_solution(14621624595101775497)
XLA Ops:
  7.2 1.3 convert_reduce_fusion
  8.5 1.3 fusion.93
  10.4 7.1 fusion.20
  17.5 5.1 copy.147
  22.6 31.3 %all_to_all.105 = bf16[3,2,96,1152]{2,1,0,3:T(2,128)(2,1)S(1)} all-to-all(bf16[3,2,96,1152]{2,1,0,3:T(2,128)(2,1)} %copy.147), channel_id=1, replica_groups=mesh['frame'=8,'pos'=16] {'pos'}, dimensions={3} | all-to-all | bytes 2654208 | tf_op jit(solution)/shard_map/all_to_all | solution.py:96
  56.0 2.5 reshape.224
  58.4 2.0 copy.150
  60.4 2.4 reshape.223
  63.7 1.7 reshape.222
  65.4 11.7 fusion.135
  77.1 10.4 fusion.57
  87.5 3.0 copy.153
  90.5 4.8 all-to-all-start.2
  96.5 12.1 all-to-all-done.2
  108.5 6.4 all-to-all-start
  114.9 3.0 copy.154
  117.9 2.1 fusion.24
  120.0 1.1 copy.156
  121.1 2.1 all-to-all-done
  124.0 4.9 all-to-all-start.3
  129.8 1.9 copy.146
  131.7 1.9 reshape.220
  133.6 3.6 all-to-all-done.3
  140.1 1.2 convert_bitcast_fusion
  141.4 2.2 multiply_reduce_fusion.4
  144.7 2.3 copy.161
  147.0 2.3 reshape.239
  149.3 6.2 convolution_convert_fusion
  156.5 2.1 copy.166
  158.6 2.1 copy.164
  161.7 4.7 fusion.136
  166.5 2.5 convolution_convert_fusion.3
  169.0 3.2 convolution_bitcast_fusion
  172.2 6.9 copy.186
  179.1 5.6 reshape.238
  185.0 3.3 convolution_convert_fusion.2
  188.3 2.1 copy.165
  190.3 3.5 fusion.137
  193.9 7.0 fusion.77
  200.8 6.9 fusion.80
  207.8 2.8 convolution_convert_fusion.4
  210.6 5.5 fusion.132
  216.1 1.1 add_convert_fusion
  217.2 1.9 reshape.233
  219.2 14.9 %all_to_all.106 = bf16[16,12,1152]{2,1,0:T(8,128)(2,1)S(1)} all-to-all(bf16[16,12,1152]{2,1,0:T(8,128)(2,1)} %reshape.233), channel_id=1, replica_groups=mesh['frame'=8,'pos'=16] {'frame'}, dimensions={0} | all-to-all | bytes 884736 | tf_op jit(solution)/shard_map/all_to_all | solution.py:108
  234.4 4.4 convolution_bitcast_fusion.1
  238.8 5.6 reshape.236
  244.4 1.6 fusion.44
  246.0 1.6 copy.174
  247.6 19.0 %all_to_all.107 = bf16[1,2,96,1152]{2,1,0,3:T(2,128)(2,1)S(1)} all-to-all(bf16[1,2,96,1152]{2,1,0,3:T(2,128)(2,1)S(1)} %copy.174), channel_id=1, replica_groups=mesh['frame'=8,'pos'=16] {'pos'}, dimensions={3} | all-to-all | bytes 884736 | tf_op jit(solution)/shard_map/all_to_all | solution.py:96
  267.5 8.0 fusion.138
  275.5 25.2 %fusion.51 = bf16[1,2,1536,1,72]{2,4,1,3,0:T(8,128)(2,1)S(1)} fusion(bf16[2,1536,72]{1,2,0:T(8,128)(2,1)S(1)} %copy-done.9, f32[2,1536,1536]{1,2,0:T(8,128)} %fusion.138, f32[2,1536,1536]{1,2,0:T(8,128)} %get-tuple-element.14, f32[2,1536]{1,0:T(2,128)S(1)} %copy-done.18), kind=kOutput, calls=%fused_computation.43 | convolution fusion | flops 712733184 | bytes 38645760 | tf_op jit(solution)/shard_map/bhlm,bmhe->blhe/dot_general | solution.py:80
  300.7 25.7 %fusion.48 = bf16[1,2,1536,1,72]{2,4,1,3,0:T(8,128)(2,1)S(1)} fusion(bf16[2,1536,72]{1,2,0:T(8,128)(2,1)S(1)} %copy-done.10, f32[2,1536,1536]{1,2,0:T(8,128)} %fusion.138, f32[2,1536,1536]{1,2,0:T(8,128)} %get-tuple-element.14, f32[2,1536]{1,0:T(2,128)S(1)} %copy-done.18), kind=kOutput, calls=%fused_computation.42 | convolution fusion | flops 712733184 | bytes 38645760 | tf_op jit(solution)/shard_map/bhlm,blhe->bmhe/dot_general | solution.py:86
  326.4 8.1 fusion.54
  334.5 1.2 maximum_bitcast_fusion
  335.7 6.3 copy.180
  342.0 34.7 %all_to_all.108 = bf16[3,2,1536,72]{3,1,0,2:T(2,128)(2,1)} all-to-all(bf16[3,2,1536,72]{3,1,0,2:T(2,128)(2,1)S(1)} %copy.180), channel_id=1, replica_groups=mesh['frame'=8,'pos'=16] {'pos'}, dimensions={2} | all-to-all | bytes 2654208 | tf_op jit(solution)/shard_map/all_to_all | solution.py:100
  376.7 6.2 copy.181
  382.9 6.2 fusion.131
  389.1 1.1 fusion.92
  390.2 435.5 %reduce-scatter.11.cloned.1.call-done = f32[1,81,128]{2,1,0:T(8,128)} async-done(((f32[128,81,128]{2,1,0:T(8,128)}), f32[1,81,128]{2,1,0:T(8,128)}) %reduce-scatter.11.cloned.1.call-update) | async-done | bytes 41488
  825.7 1.4 reshape_reduce_scatter.7
  827.2 641.4 %reduce-scatter.9.cloned.1.call-done = f32[1,81,128]{2,1,0:T(8,128)} async-done(((f32[128,81,128]{2,1,0:T(8,128)}), f32[1,81,128]{2,1,0:T(8,128)}) %reduce-scatter.9.cloned.1.call-update) | async-done | bytes 41488
  1468.6 1.4 reshape_reduce_scatter.6
  (70 shorter events, 13.9 us)
Async XLA Ops:
  7.2 110.7 %copy-start = (bf16[1152,1152]{1,0:T(8,128)(2,1)S(1)}, bf16[1152,1152]{1,0:T(8,128)(2,1)}, u32[]{:S(2)}) copy-start(bf16[1152,1152]{1,0:T(8,128)(2,1)} %param.9) | copy-start | bytes 7962628
  8.5 1.3 copy-start.11
  9.8 0.6 copy-start.13
  65.4 11.7 copy-start.5
  77.1 10.4 copy-start.17
  77.1 18.2 %copy-start.8 = (bf16[2,96,1152]{2,1,0:T(8,128)(2,1)S(1)}, bf16[2,96,1152]{2,1,0:T(8,128)(2,1)}, u32[]{:S(2)}) copy-start(bf16[2,96,1152]{2,1,0:T(8,128)(2,1)} %param.7) | copy-start | bytes 1327108
  87.5 30.3 %copy-start.2 = (bf16[2,96,1152]{2,1,0:T(8,128)(2,1)S(1)}, bf16[2,96,1152]{2,1,0:T(8,128)(2,1)}, u32[]{:S(2)}) copy-start(bf16[2,96,1152]{2,1,0:T(8,128)(2,1)} %param.6) | copy-start | bytes 1327108
  90.5 18.0 %all-to-all-start.2 = ((bf16[1,2,1536,72]{3,1,0,2:T(2,128)(2,1)}), bf16[1,2,1536,72]{3,1,0,2:T(2,128)(2,1)}, u32[]{:S(2)}, u32[]{:S(2)}) async-start(bf16[1,2,1536,72]{3,1,0,2:T(2,128)(2,1)} %copy.153), calls=%async_computation.2 | async-start | bytes 1572864 | tf_op jit(solution)/shard_map/all_to_all | solution.py:100
  108.5 14.7 all-to-all-start
  123.2 0.8 copy-start.7
  124.0 13.3 all-to-all-start.3
  128.9 696.8 %reduce-scatter.11.cloned.1.call-start = ((), (), s32[]{:S(2)}) async-start(), calls=%async_computation.10 | async-start | bytes 5812224
  166.5 2.5 copy-start.3
  184.7 1283.9 %reduce-scatter.9.cloned.1.call-start = ((), (), s32[]{:S(2)}) async-start(), calls=%async_computation.9 | async-start | bytes 5812224
  207.8 2.8 copy-start.4
  207.8 2.8 copy-start.15
  207.8 2.8 copy-start.16
  246.0 21.4 %copy-start.6 = (bf16[2,1536,72]{1,2,0:T(8,128)(2,1)S(1)}, bf16[2,1536,72]{1,2,0:T(8,128)(2,1)}, u32[]{:S(2)}) copy-start(bf16[2,1536,72]{1,2,0:T(8,128)(2,1)} %copy-done.5) | copy-start | bytes 1327108
  267.5 8.0 copy-start.9
  267.5 8.0 copy-start.18
  275.5 25.3 %copy-start.10 = (bf16[2,1536,72]{1,2,0:T(8,128)(2,1)S(1)}, bf16[2,1536,72]{1,2,0:T(8,128)(2,1)}, u32[]{:S(2)}) copy-start(bf16[2,1536,72]{1,2,0:T(8,128)(2,1)} %reshape.223) | copy-start | bytes 1327108
  376.7 6.2 copy-start.12
  376.7 6.2 copy-start.14
  382.9 1087.1 %copy-start.1 = (bf16[1152,1152]{1,0:T(8,128)(2,1)S(1)}, bf16[1152,1152]{1,0:T(8,128)(2,1)}, u32[]{:S(2)}) copy-start(bf16[1152,1152]{1,0:T(8,128)(2,1)} %param.9) | copy-start | bytes 7962628
Sparse Core Ops, SparseCore 0:
  184.8 640.8 reduce-scatter.10
  828.2 640.3 reduce-scatter.8

commit v2 on v0

v2 whole, which is shorter than its diff:
```python
import jax
import jax.numpy as jnp
import numpy as np
from jax import lax
from jax.experimental import pallas as pl
from jax.experimental.pallas import tpu as pltpu
from jax.sharding import PartitionSpec as P

HEADS = 16
EPS = 1e-06
BF = jnp.bfloat16
F32 = jnp.float32
D = 1152
HD = 72
NP = 16
NF = 8
FR = 2
PL = 96
TOK = FR * PL
ALL = NP * PL
TP = PL // NF
SLAB = 32
TT = NF * SLAB
GR = D // NF
SCALE = HD ** (-0.5)
LOG2E = 1.4426950408889634
QT = 384
BT = 256
KC = 256
LIMIT = 60 * 1024 * 1024


def dot(a, b, ca, cb):
    return lax.dot_general(a, b, (((ca,), (cb,)), ((), ())), preferred_element_type=F32)


def normalize(tokens):
    values = tokens.astype(F32)
    center = values - jnp.mean(values, axis=-1, keepdims=True)
    inv_std = lax.rsqrt(jnp.mean(center * center, axis=-1, keepdims=True) + EPS)
    return center * inv_std, inv_std


def norm_back(grad_hat, normed, inv_std):
    mean_grad = jnp.mean(grad_hat, axis=-1, keepdims=True)
    mean_proj = jnp.mean(grad_hat * normed, axis=-1, keepdims=True)
    return inv_std * (grad_hat - mean_grad - normed * mean_proj)


def greet(barrier, p, f, pos, frame):
    if pos:

        @pl.loop(1, NP)
        def _(s):
            pl.semaphore_signal(barrier, inc=1, device_id={"pos": lax.rem(p + s, NP)})

    if frame:

        @pl.loop(1, NF)
        def _(s):
            pl.semaphore_signal(barrier, inc=1, device_id={"frame": lax.rem(f + s, NF)})


def send(src, dst, send_sem, recv_sem, axis, dest):
    return pltpu.make_async_remote_copy(
        src_ref=src, dst_ref=dst, send_sem=send_sem, recv_sem=recv_sem, device_id={axis: dest}
    )


def space_forward_kernel(
    x, cot, perm, w_hbm, so_hbm,
    qkv_out, stat_out, att_out, mixed_out, stream_out, cot_out,
    w, so, hat, qsend, qkv, kbuf, qbuf, vt, sbuf, pbuf, osend, orecv, stream, fsend, frecv, csend, crecv,
    wsem, sosem, qss, qrs, oss, ors, fss, frs, css, crs, outsem,
):
    p = lax.axis_index("pos")
    f = lax.axis_index("frame")
    par = lax.rem(p, 2)
    half = p // 2
    barrier = pltpu.get_barrier_semaphore()
    greet(barrier, p, f, True, True)

    def w_copy(i, c):
        pair = lax.rem(half + i, 8)
        rows = pl.ds(pl.multiple_of(c * D + pair * 144, 16), 144)
        return pltpu.make_async_copy(w_hbm.at[rows], w.at[i, pl.ds(c * 144, 144)], wsem.at[i, c])

    for i in range(8):
        for c in range(3):
            w_copy(i, c).start()
    so_copy = pltpu.make_async_copy(so_hbm, so, sosem)
    so_copy.start()
    hat[...] = normalize(x[...])[0].astype(BF)
    pl.semaphore_wait(barrier, NP - 1 + NF - 1)

    def peer(s, sign):
        pair = lax.rem(half + sign * (s // 2) + 8, 8)
        return 2 * pair + lax.rem(par + s, 2)

    def q_copy(fr, s):
        return send(qsend.at[s, fr], qkv.at[fr, p], qss.at[fr, s], qrs.at[fr, s], "pos", peer(s, 1))

    @pl.loop(0, 8)
    def _(i):
        for c in range(3):
            w_copy(i, c).wait()
        r = dot(hat[...], w[i], 1, 1)
        pad = jnp.zeros((TOK, 256 - 3 * HD), F32)
        for e in range(2):
            part = [r[:, c * 144 + e * HD : c * 144 + e * HD + HD] for c in range(3)]
            val = jnp.concatenate(part + [pad], axis=1).astype(BF)
            qsend[2 * i + lax.rem(par + e, 2)] = val.reshape(FR, PL, 256)

        @pl.when(i > 0)
        def _():
            q_copy(0, 2 * i).start()

        q_copy(0, 2 * i + 1).start()

    @pl.loop(1, NP)
    def _(s):
        q_copy(1, s).start()

    qkv[:, pl.ds(p, 1)] = qsend[0][:, None]

    def c_copy(s):
        to = lax.rem(f + s, NF)
        return send(csend.at[to], crecv.at[f], css.at[s], crs.at[s], "frame", to)

    csend[...] = dot(perm[...], cot[...], 1, 0).astype(BF).reshape(NF, SLAB, D)

    @pl.loop(1, NF)
    def _(s):
        c_copy(s).start()

    crecv[pl.ds(f, 1)] = csend[pl.ds(f, 1)]

    def o_copy(fr, s):
        to = lax.rem(p + s, NP)
        return send(osend.at[fr, to], orecv.at[fr, p], oss.at[fr, s], ors.at[fr, s], "pos", to)

    outs = []
    for fr in range(FR):

        @pl.loop(1, NP)
        def _(s):
            q_copy(fr, s).wait_recv()

        out = pltpu.make_async_copy(qkv.at[fr], qkv_out.at[fr], outsem.at[fr])
        out.start()
        outs.append(out)
        rows = qkv[fr].reshape(ALL, 256)
        lane = lax.broadcasted_iota(jnp.int32, (1, 128), 1)
        keep = (lane < HD).astype(F32).astype(BF)
        zeros = jnp.zeros((ALL, 128 - HD), BF)
        qbuf[...] = rows[:, :128] * keep
        kbuf[...] = rows[:, HD : HD + 128]
        vt[...] = jnp.concatenate([rows[:, 2 * HD : 3 * HD], zeros], axis=1).T

        @pl.loop(0, ALL // QT)
        def _(t):
            tile = lax.rem(p // 4 + t, ALL // QT)
            at = pl.ds(pl.multiple_of(tile * QT, QT), QT)
            q = qbuf[at]
            top = jnp.full((8, QT), -jnp.inf, F32)
            for k in range(0, ALL, KC):
                s = dot(kbuf[k : k + KC], q, 1, 1)
                sbuf[k : k + KC] = s
                top = jnp.maximum(top, jnp.max(s.reshape(KC // 8, 8, QT), axis=0))
            top = jnp.max(top, axis=0, keepdims=True) * (SCALE * LOG2E)
            total = jnp.zeros((8, QT), F32)
            for k in range(0, ALL, KC):
                e = jnp.exp2(sbuf[k : k + KC] * (SCALE * LOG2E) - top)
                total = total + jnp.sum(e.reshape(KC // 8, 8, QT), axis=0)
                pbuf[k : k + KC] = e.astype(BF)
            total = jnp.sum(total, axis=0, keepdims=True)
            o = dot(vt[...], pbuf[...], 1, 0) * (1.0 / total)
            stat_out[fr, :, at] = jnp.broadcast_to(top + jnp.log(total) * LOG2E, (8, QT))
            att_out[fr, :, at] = o
            osend[fr, pl.ds(tile * 4, 4)] = o.T.astype(BF).reshape(4, PL, 128)
            for j in range(4):
                to = tile * 4 + j

                @pl.when(to != p)
                def _():
                    o_copy(fr, lax.rem(to - p + NP, NP)).start()

        orecv[fr, pl.ds(p, 1)] = osend[fr, pl.ds(p, 1)]

    so_copy.wait()
    for fr in range(FR):

        @pl.loop(1, NP)
        def _(s):
            o_copy(fr, s).wait_recv()

        mixed = jnp.concatenate([orecv[fr, h][:, :HD].astype(F32) for h in range(HEADS)], axis=1)
        mixed = mixed.astype(BF)
        part = slice(fr * PL, (fr + 1) * PL)
        mixed_out[part] = mixed
        stream[part] = (x[part].astype(F32) + dot(mixed, so[...], 1, 1)).astype(BF)

    def f_copy(s):
        to = lax.rem(f + s, NF)
        return send(fsend.at[to], frecv.at[f], fss.at[s], frs.at[s], "frame", to)

    fsend[...] = dot(perm[...], stream[...], 1, 0).astype(BF).reshape(NF, SLAB, D)

    @pl.loop(1, NF)
    def _(s):
        f_copy(s).start()

    frecv[pl.ds(f, 1)] = fsend[pl.ds(f, 1)]

    @pl.loop(1, NF)
    def _(s):
        c_copy(s).wait_recv()

    cot_out[...] = crecv[...]

    @pl.loop(1, NP)
    def _(s):
        for fr in range(FR):
            q_copy(fr, s).wait_send()
            o_copy(fr, s).wait_send()

    for out in outs:
        out.wait()

    @pl.loop(1, NF)
    def _(s):
        f_copy(s).wait_recv()

    stream_out[...] = frecv[...]

    @pl.loop(1, NF)
    def _(s):
        c_copy(s).wait_send()
        f_copy(s).wait_send()


def vmem():
    return pl.BlockSpec(memory_space=pltpu.VMEM)


def anywhere():
    return pl.BlockSpec(memory_space=pl.ANY)


DMA = pltpu.SemaphoreType.DMA


def params(collective_id):
    return pltpu.CompilerParams(
        collective_id=collective_id, has_side_effects=True, vmem_limit_bytes=LIMIT
    )


def space_forward(x, cot, perm, w, so):
    V = pltpu.VMEM
    sds = jax.ShapeDtypeStruct
    return pl.pallas_call(
        space_forward_kernel,
        out_shape=(
            sds((FR, NP, PL, 256), BF),
            sds((FR, 8, ALL), F32),
            sds((FR, 128, ALL), F32),
            sds((TOK, D), BF),
            sds((NF, SLAB, D), BF),
            sds((NF, SLAB, D), BF),
        ),
        in_specs=[vmem(), vmem(), vmem(), anywhere(), anywhere()],
        out_specs=(anywhere(), vmem(), vmem(), vmem(), vmem(), vmem()),
        scratch_shapes=[
            V((8, 432, D), BF), V((D, D), BF), V((TOK, D), BF), V((NP, FR, PL, 256), BF),
            V((FR, NP, PL, 256), BF), V((ALL, 128), BF), V((ALL, 128), BF), V((128, ALL), BF),
            V((ALL, QT), F32), V((ALL, QT), BF),
            V((FR, NP, PL, 128), BF), V((FR, NP, PL, 128), BF), V((TOK, D), BF),
            V((NF, SLAB, D), BF), V((NF, SLAB, D), BF), V((NF, SLAB, D), BF), V((NF, SLAB, D), BF),
            DMA((8, 3)), DMA, DMA((FR, NP)), DMA((FR, NP)), DMA((FR, NP)), DMA((FR, NP)),
            DMA((NF,)), DMA((NF,)), DMA((NF,)), DMA((NF,)), DMA((FR,)),
        ],
        compiler_params=params(1),
    )(x, cot, perm, w, so)


def time_kernel(
    stream, cot, mask, unperm, w_hbm, to_hbm,
    up_out, grad_out,
    w, wo, hat, qkv, back, mixed, dqkv, usend, urecv,
    wsem, tosem, uss, urs,
):
    p = lax.axis_index("pos")
    f = lax.axis_index("frame")
    barrier = pltpu.get_barrier_semaphore()
    greet(barrier, p, f, False, True)
    to_copy = pltpu.make_async_copy(to_hbm, wo, tosem)
    to_copy.start()
    w_copies = [pltpu.make_async_copy(w_hbm.at[pl.ds(c * D, D)], w.at[c], wsem.at[c]) for c in range(3)]
    for c in w_copies:
        c.start()
    normed, inv = normalize(stream[...])
    hat[...] = normed
    normed = normed.astype(BF)
    to_copy.wait()
    back[...] = dot(cot[...], wo[...], 1, 0).astype(BF)
    for c in range(3):
        w_copies[c].wait()
        qkv[c] = dot(normed, w[c], 1, 1).astype(BF)
    mixed[...] = jnp.zeros_like(mixed)
    dqkv[...] = jnp.zeros_like(dqkv)
    for h in range(HEADS):
        off = (h * HD) % 128
        start = h * HD - off
        width = 128 if off + HD <= 128 else 256
        win = slice(start, start + width)
        lane = lax.broadcasted_iota(jnp.int32, (1, width), 1)
        keep = ((lane >= off) & (lane < off + HD)).astype(F32).astype(BF)
        q, k, v, b = qkv[0, :, win], qkv[1, :, win], qkv[2, :, win], back[:, win]
        qm, km, vm, bm = q * keep, k * keep, v * keep, b * keep
        s = dot(qm, k, 1, 1) * SCALE + mask[...]
        e = jnp.exp(s - jnp.max(s, axis=1, keepdims=True))
        prob = e * (1.0 / jnp.sum(e, axis=1, keepdims=True))
        pb = prob.astype(BF)
        mixed[:, win] += dot(pb, vm, 1, 0)
        gp = dot(bm, v, 1, 1)
        gs = prob * (gp - jnp.sum(prob * gp, axis=1, keepdims=True)) * SCALE
        gs = gs.astype(BF)
        dqkv[0, :, win] += dot(gs, km, 1, 0)
        dqkv[1, :, win] += dot(gs, qm, 0, 0)
        dqkv[2, :, win] += dot(pb, bm, 0, 0)
    grad_hat = dot(dqkv[0].astype(BF), w[0], 1, 0)
    for c in range(1, 3):
        grad_hat += dot(dqkv[c].astype(BF), w[c], 1, 0)
    up = cot[...].astype(F32) + norm_back(grad_hat, hat[...], inv)
    usend[...] = up.astype(BF).reshape(NF, SLAB, D)
    pl.semaphore_wait(barrier, NF - 1)

    def u_copy(s):
        to = lax.rem(f + s, NF)
        return send(usend.at[to], urecv.at[f], uss.at[s], urs.at[s], "frame", to)

    @pl.loop(1, NF)
    def _(s):
        u_copy(s).start()

    urecv[pl.ds(f, 1)] = usend[pl.ds(f, 1)]
    mb = mixed[...].astype(BF)
    for r in range(0, D, 128):
        grad_out[r : r + 128] = dot(cot[:, r : r + 128], mb, 0, 0).astype(BF)

    @pl.loop(1, NF)
    def _(s):
        u_copy(s).wait()

    up_out[...] = dot(unperm[...], urecv[...].reshape(TT, D), 1, 0).astype(BF)


def time_block(stream, cot, mask, unperm, w, wo):
    V = pltpu.VMEM
    sds = jax.ShapeDtypeStruct
    return pl.pallas_call(
        time_kernel,
        out_shape=(sds((TOK, D), BF), sds((D, D), BF)),
        in_specs=[vmem(), vmem(), vmem(), vmem(), anywhere(), anywhere()],
        out_specs=(vmem(), vmem()),
        scratch_shapes=[
            V((3, D, D), BF), V((D, D), BF), V((TT, D), F32), V((3, TT, D), BF), V((TT, D), BF),
            V((TT, D), F32), V((3, TT, D), F32), V((NF, SLAB, D), BF), V((NF, SLAB, D), BF),
            DMA((3,)), DMA, DMA((NF,)), DMA((NF,)),
        ],
        compiler_params=params(2),
    )(stream, cot, mask, unperm, w, wo)


def space_backward_kernel(
    x, up, mixed, spread, stat, att, qkv_hbm, gt_hbm, w_hbm, so_hbm,
    grad_out, gs_out, gt_out,
    w, so, qkv, bsend, brecv, gpart, grecv, hsend, hrecv, qbuf, kbuf, vbuf, kt, pbuf, sbuf,
    dq, dk, dv, rsend, rrecv,
    wsem, sosem, qsem, gsem, bss, brs, gss, grs, hss, hrs, rss, rrs,
):
    p = lax.axis_index("pos")
    f = lax.axis_index("frame")
    barrier = pltpu.get_barrier_semaphore()
    greet(barrier, p, f, True, True)
    so_copy = pltpu.make_async_copy(so_hbm, so, sosem)
    so_copy.start()
    qkv_copy = pltpu.make_async_copy(qkv_hbm, qkv, qsem)
    qkv_copy.start()
    gt_copy = pltpu.make_async_copy(gt_hbm, gpart.at[0], gsem)
    gt_copy.start()
    w_copy = pltpu.make_async_copy(w_hbm, w, wsem)
    w_copy.start()
    so_copy.wait()
    back = dot(up[...], so[...], 1, 0)
    pad = jnp.zeros((TOK, 128 - HD), F32)
    for h in range(HEADS):
        val = jnp.concatenate([back[:, h * HD : (h + 1) * HD], pad], axis=1).astype(BF)
        bsend[:, h] = val.reshape(FR, PL, 128)
    pl.semaphore_wait(barrier, NP - 1 + NF - 1)

    def b_copy(fr, s):
        to = lax.rem(p + s, NP)
        return send(bsend.at[fr, to], brecv.at[fr, p], bss.at[fr, s], brs.at[fr, s], "pos", to)

    for fr in range(FR):

        @pl.loop(1, NP)
        def _(s):
            b_copy(fr, s).start()

    brecv[:, pl.ds(p, 1)] = bsend[:, pl.ds(p, 1)]

    def g_copy(g, s):
        to = lax.rem(f + s, NF)
        rows = pl.ds(pl.multiple_of(to * GR, 16), GR)
        return send(gpart.at[g, rows], grecv.at[g, f], gss.at[g, s], grs.at[g, s], "frame", to)

    gt_copy.wait()

    @pl.loop(1, NF)
    def _(s):
        g_copy(0, s).start()

    for r in range(0, D, 128):
        gpart[1, r : r + 128] = dot(up[:, r : r + 128], mixed[...], 0, 0).astype(BF)

    @pl.loop(1, NF)
    def _(s):
        g_copy(1, s).start()

    for g in range(2):
        grecv[g, pl.ds(f, 1)] = gpart[g, pl.ds(pl.multiple_of(f * GR, 16), GR)][None]

    def r_copy(fr, s):
        to = lax.rem(p + s, NP)
        return send(rsend.at[fr, to], rrecv.at[fr, p], rss.at[fr, s], rrs.at[fr, s], "pos", to)

    qkv_copy.wait()
    lane = lax.broadcasted_iota(jnp.int32, (1, 128), 1)
    keep = (lane < HD).astype(F32).astype(BF)
    for fr in range(FR):
        rows = qkv[fr].reshape(ALL, 256)
        zeros = jnp.zeros((ALL, 128 - HD), BF)
        qbuf[...] = rows[:, :128] * keep
        k = rows[:, HD : HD + 128] * keep
        kbuf[...] = k
        kt[...] = k.T
        vbuf[...] = jnp.concatenate([rows[:, 2 * HD : 3 * HD], zeros], axis=1)
        dk[...] = jnp.zeros_like(dk)
        dv[...] = jnp.zeros_like(dv)

        @pl.loop(1, NP)
        def _(s):
            b_copy(fr, s).wait_recv()

        @pl.loop(0, ALL // BT)
        def _(t):
            at = pl.ds(pl.multiple_of(t * BT, BT), BT)
            q = qbuf[at]
            b = brecv.reshape(FR, ALL, 128)[fr, at]
            total = jnp.sum(b.astype(F32).T * att[fr, :, at], axis=0, keepdims=True)
            lse = stat[fr, 0:1, at]
            for k in range(0, ALL, KC):
                s = dot(kbuf[k : k + KC], q, 1, 1)
                gp = dot(vbuf[k : k + KC], b, 1, 1)
                prob = jnp.exp2(s * (SCALE * LOG2E) - lse)
                pbuf[k : k + KC] = prob.astype(BF)
                sbuf[k : k + KC] = (prob * (gp - total)).astype(BF)
            dv[...] += dot(pbuf[...], b, 1, 0)
            dk[...] += dot(sbuf[...], q, 1, 0)
            dq[at] = dot(kt[...], sbuf[...], 1, 0).T

        val = jnp.concatenate(
            [
                dq[:, :HD] * SCALE,
                dk[:, :HD] * SCALE,
                dv[:, :HD],
                jnp.zeros((ALL, 256 - 3 * HD), F32),
            ],
            axis=1,
        )
        rsend[fr] = val.astype(BF).reshape(NP, PL, 256)

        @pl.loop(1, NP)
        def _(s):
            r_copy(fr, s).start()

        rrecv[fr, pl.ds(p, 1)] = rsend[fr, pl.ds(p, 1)]

    def h_copy(g, s):
        to = lax.rem(p + s, NP)
        return send(hsend.at[g, to], hrecv.at[g, p], hss.at[g, s], hrs.at[g, s], "pos", to)

    for g in range(2):

        @pl.loop(1, NF)
        def _(s):
            g_copy(g, s).wait_recv()

        total = grecv[g, 0].astype(F32)
        for s in range(1, NF):
            total += grecv[g, s].astype(F32)
        hsend[g] = dot(spread[...], total.astype(BF), 1, 0).astype(BF).reshape(NP, 16, D)

        @pl.loop(1, NP)
        def _(s):
            h_copy(g, s).start()

        hrecv[g, pl.ds(p, 1)] = hsend[g, pl.ds(p, 1)]

    w_copy.wait()
    for fr in range(FR):

        @pl.loop(1, NP)
        def _(s):
            r_copy(fr, s).wait_recv()

        got = [rrecv[fr, h].astype(F32) for h in range(HEADS)]
        grad_hat = jnp.zeros((PL, D), F32)
        for c in range(3):
            part = jnp.concatenate([v[:, c * HD : (c + 1) * HD] for v in got], axis=1)
            grad_hat += dot(part.astype(BF), w[c * D : (c + 1) * D], 1, 0)
        here = slice(fr * PL, (fr + 1) * PL)
        normed, inv = normalize(x[here])
        grad_out[here] = (up[here].astype(F32) + norm_back(grad_hat, normed, inv)).astype(BF)

    for g, out in ((0, gt_out), (1, gs_out)):

        @pl.loop(1, NP)
        def _(s):
            h_copy(g, s).wait_recv()

        total = hrecv[g, 0].astype(F32)
        for s in range(1, NP):
            total += hrecv[g, s].astype(F32)
        out[...] = total

    @pl.loop(1, NP)
    def _(s):
        for fr in range(FR):
            b_copy(fr, s).wait_send()
            r_copy(fr, s).wait_send()
        for g in range(2):
            h_copy(g, s).wait_send()

    @pl.loop(1, NF)
    def _(s):
        for g in range(2):
            g_copy(g, s).wait_send()


def space_backward(x, up, mixed, spread, stat, att, qkv, gt, w, so):
    V = pltpu.VMEM
    sds = jax.ShapeDtypeStruct
    return pl.pallas_call(
        space_backward_kernel,
        out_shape=(sds((TOK, D), BF), sds((16, D), F32), sds((16, D), F32)),
        in_specs=[vmem()] * 6 + [anywhere()] * 4,
        out_specs=(vmem(), vmem(), vmem()),
        scratch_shapes=[
            V((3 * D, D), BF), V((D, D), BF), V((FR, NP, PL, 256), BF),
            V((FR, NP, PL, 128), BF), V((FR, NP, PL, 128), BF),
            V((2, D, D), BF), V((2, NF, GR, D), BF), V((2, NP, 16, D), BF), V((2, NP, 16, D), BF),
            V((ALL, 128), BF), V((ALL, 128), BF), V((ALL, 128), BF), V((128, ALL), BF),
            V((ALL, BT), BF), V((ALL, BT), BF),
            V((ALL, 128), F32), V((ALL, 128), F32), V((ALL, 128), F32),
            V((FR, NP, PL, 256), BF), V((FR, NP, PL, 256), BF),
            DMA, DMA, DMA, DMA, DMA((FR, NP)), DMA((FR, NP)), DMA((2, NF)), DMA((2, NF)),
            DMA((2, NP)), DMA((2, NP)), DMA((FR, NP)), DMA((FR, NP)),
        ],
        compiler_params=params(3),
    )(x, up, mixed, spread, stat, att, qkv, gt, w, so)


def tables():
    row = np.arange(TT)
    slab, inner = row // SLAB, row % SLAB
    real = inner < FR * TP
    col = (inner // TP) * PL + slab * TP + inner % TP
    perm = (real[:, None] & (col[:, None] == np.arange(TOK)[None])).astype(np.float32)
    place = np.where(real, inner % TP, -1)
    mask = np.where(place[:, None] == place[None], 0.0, -1e30).astype(np.float32)
    row = np.arange(NP * 16)
    spread = (row % 16 < GR // NP)[:, None] & (
        ((row // 16) * (GR // NP) + row % 16)[:, None] == np.arange(GR)[None]
    )
    return jnp.asarray(perm, BF), jnp.asarray(perm.T, BF), jnp.asarray(mask), jnp.asarray(spread, BF)


def shards(inputs, cotangent, space_projection, space_output, time_projection, time_output):
    perm, unperm, mask, spread = tables()
    x = inputs.reshape(TOK, D)
    cot = cotangent.reshape(TOK, D)
    qkv, stat, att, mixed, stream_t, cot_t = space_forward(x, cot, perm, space_projection, space_output)
    up, gt = time_block(
        stream_t.reshape(TT, D), cot_t.reshape(TT, D), mask, unperm, time_projection, time_output
    )
    grad, gs, gt = space_backward(
        x, up, mixed, spread, stat, att, qkv, gt, space_projection, space_output
    )
    rows = GR // NP
    return grad.reshape(FR, PL, D), gs[:rows], gt[:rows]


def solution(mesh):
    return jax.shard_map(
        shards,
        mesh=mesh,
        in_specs=(P("frame", "pos", None), P("frame", "pos", None), P(), P(), P(), P()),
        out_specs=(P("frame", "pos", None), P(("frame", "pos"), None), P(("frame", "pos"), None)),
        check_vma=False,
    )
```

time: 456 us -> 220 us (0.48); the launches traced: 448 us -> 219 us
  Pallas kernels: 0 us -> 214 us
  matrix products: 151 us -> 0 us
  waiting for transfers between devices: 111 us -> 0 us
  local copies, waits for them, and re-layouts: 80.4 us -> 4.85 us
  blocking collectives: 49.5 us -> 0 us
  starting transfers between devices: 34.7 us -> 0 us
  between operations: 14.6 us -> 0.66 us
  other arithmetic: 7.4 us -> 0 us
    pallas_call x0 -> x3, Pallas kernels: none -> 214 us  [the longest x1 123 us: space_backward(): pl.pallas_call(space_backward_kernel, out_shape=(sds((TOK, D), BF), sds((...]
    dot_general x19 -> x0, matrix products: 136 us -> none  [the longest x2 31.9 us: attend_back(): jnp.einsum('bhlm,' + key_form + '->' + token_form, grad_scores, key_vecto...]
    all_to_all x6 -> x0, waiting for transfers between devices: 77.5 us -> none  [the longest x2 42.9 us: space_rows(): lax.all_to_all(stacked, 'pos', split_axis=2, concat_axis=3, tiled=True)]
    all_to_all x2 -> x0, blocking collectives: 49.5 us -> none  [space_heads(): lax.all_to_all(stacked, 'pos', split_axis=3, concat_axis=2, tiled=True)]
    all_to_all x6 -> x0, starting transfers between devices: 34.6 us -> none  [the longest x2 13.5 us: time_heads(): lax.all_to_all(stacked, 'frame', split_axis=3, concat_axis=1, tiled=True)]
    unnamed x2 -> x0, waiting for transfers between devices: 33 us -> none
    convert_element_type x6 -> x0, local copies, waits for them, and re-layouts: 21 us -> none  [the longest x2 10.2 us: project_in(): return result.astype(jnp.bfloat16)]
    sub x2 -> x0, matrix products: 15.4 us -> none  [attend(): probability = jax.nn.softmax(scores * score_scale, axis=-1)]
  transfers between devices with their start and end apart: 7 -> 0, of which waited for: 5 -> 0; matrix products, arithmetic and copies ran while one was open for 30% -> 0% of each run, Pallas kernels for 0% -> 0%
where the time goes in v2:
time: 220 us; the launch traced here: 219 us
  Pallas kernels  214 us (97%)
  local copies, waits for them, and re-layouts  4.85 us (2%)
    pallas_call x1, Pallas kernels, space_backward(): pl.pallas_call(space_backward_kernel, out_shape=(sds((TOK, D), BF), sds((...  123 us
    pallas_call x1, Pallas kernels, space_forward(): pl.pallas_call(space_forward_kernel, out_shape=(sds((FR, NP, PL, 256), BF...  57.3 us
    pallas_call x1, Pallas kernels, time_block(): pl.pallas_call(time_kernel, out_shape=(sds((TOK, D), BF), sds((D, D), BF)...  33.7 us
    unnamed x3, local copies, waits for them, and re-layouts  4.85 us

profile of v2, /device:TPU:1, one launch (start us, length us, event | category | flops | bytes accessed | tf_op | source)
XLA Modules:
  0.0 219.1 jit_solution(11326641299319073065)
XLA Ops:
  0.6 57.3 %shard_map.121 = (bf16[2,16,96,256]{3,2,1,0:T(8,128)(2,1)}, f32[2,8,1536]{2,1,0:T(8,128)}, f32[2,128,1536]{2,1,0:T(8,128)}, bf16[192,1152]{1,0:T(8,128)(2,1)}, b...) custom-call(bf16[192,1152]{1,0:T(8,128)(2,1)} %bitcast.7, bf16[192,1152]{1,0:T(8,128)(2,1)} %bitcast.12, ...), custom_call_target="tpu_custom_call" | custom-call | tf_op jit(solution)/shard_map/pallas_call | solution.py:262
  58.0 33.7 %shard_map.122 = (bf16[192,1152]{1,0:T(8,128)(2,1)}, bf16[1152,1152]{1,0:T(8,128)(2,1)}) custom-call(bf16[256,1152]{1,0:T(8,128)(2,1)} %bitcast.9, bf16[256,1152]{1,0:T(8,128)(2,1)} %bitcast.10, f32[256,256]{1,0:T(8,128)} %constant.10.clone.mask, bf16[192,256]{1,0:T(8,128)(2,1)} %constant.9.clone.unperm, bf16[3456,1152]{1,0:T(8,128)(2,1)} %w_hbm.4, ...), custom_call_target="tpu_custom_call" | custom-call | tf_op jit(solution)/shard_map/pallas_call | solution.py:362
  91.7 122.5 %shard_map.123 = (bf16[192,1152]{1,0:T(8,128)(2,1)}, f32[16,1152]{1,0:T(8,128)}, f32[16,1152]{1,0:T(8,128)}) custom-call(bf16[192,1152]{1,0:T(8,128)(2,1)} %bitcast.8, bf16[192,1152]{1,0:T(8,128)(2,1)} %get-tuple-element.16.up, bf16[192,1152]{1,0:T(8,128)(2,1)} %get-tuple-element.17.mixed, bf16[256,144]{1,0:T(8,128)(2,1)} %constant.11.clone.spread, ...), custom_call_target="tpu_custom_call" | custom-call | tf_op jit(solution)/shard_map/pallas_call | solution.py:557
  214.2 1.8 copy.16
  216.0 1.5 copy.17
  217.6 1.5 copy.18

commit v3 on v2

--- a/solution.py
+++ b/solution.py
@@ -21,7 +21,11 @@
 TP = PL // NF
 SLAB = 32
 TT = NF * SLAB
-GR = D // NF
+GR = D // NF // NP
+NK = NP // 2
+GS = 80
+GH = NF * GS
+GRP = PL // 3
 SCALE = HD ** (-0.5)
 LOG2E = 1.4426950408889634
 QT = 384
@@ -45,6 +49,15 @@
     mean_grad = jnp.mean(grad_hat, axis=-1, keepdims=True)
     mean_proj = jnp.mean(grad_hat * normed, axis=-1, keepdims=True)
     return inv_std * (grad_hat - mean_grad - normed * mean_proj)
+
+
+def pack(parts):
+    shape = parts[0].shape[:-1] + (256 - 3 * HD,)
+    return jnp.concatenate(list(parts) + [jnp.zeros(shape, F32)], axis=-1).astype(BF)
+
+
+def lanes(value, g):
+    return value[..., g * HD : (g + 1) * HD]
 
 
 def greet(barrier, p, f, pos, frame):
@@ -177,7 +190,8 @@
             o = dot(vt[...], pbuf[...], 1, 0) * (1.0 / total)
             stat_out[fr, :, at] = jnp.broadcast_to(top + jnp.log(total) * LOG2E, (8, QT))
             att_out[fr, :, at] = o
-            osend[fr, pl.ds(tile * 4, 4)] = o.T.astype(BF).reshape(4, PL, 128)
+            turned = o.T.reshape(4, 3, GRP, 128)
+            osend[fr, pl.ds(tile * 4, 4)] = pack([turned[:, g, :, :HD] for g in range(3)])
             for j in range(4):
                 to = tile * 4 + j
 
@@ -194,8 +208,10 @@
         def _(s):
             o_copy(fr, s).wait_recv()
 
-        mixed = jnp.concatenate([orecv[fr, h][:, :HD].astype(F32) for h in range(HEADS)], axis=1)
-        mixed = mixed.astype(BF)
+        got = [orecv[fr, h].astype(F32) for h in range(HEADS)]
+        mixed = jnp.concatenate(
+            [jnp.concatenate([lanes(v, g) for v in got], axis=1) for g in range(3)], axis=0
+        ).astype(BF)
         part = slice(fr * PL, (fr + 1) * PL)
         mixed_out[part] = mixed
         stream[part] = (x[part].astype(F32) + dot(mixed, so[...], 1, 1)).astype(BF)
@@ -275,7 +291,7 @@
             V((8, 432, D), BF), V((D, D), BF), V((TOK, D), BF), V((NP, FR, PL, 256), BF),
             V((FR, NP, PL, 256), BF), V((ALL, 128), BF), V((ALL, 128), BF), V((128, ALL), BF),
             V((ALL, QT), F32), V((ALL, QT), BF),
-            V((FR, NP, PL, 128), BF), V((FR, NP, PL, 128), BF), V((TOK, D), BF),
+            V((FR, NP, GRP, 256), BF), V((FR, NP, GRP, 256), BF), V((TOK, D), BF),
             V((NF, SLAB, D), BF), V((NF, SLAB, D), BF), V((NF, SLAB, D), BF), V((NF, SLAB, D), BF),
             DMA((8, 3)), DMA, DMA((FR, NP)), DMA((FR, NP)), DMA((FR, NP)), DMA((FR, NP)),
             DMA((NF,)), DMA((NF,)), DMA((NF,)), DMA((NF,)), DMA((FR,)),
@@ -285,20 +301,25 @@
 
 
 def time_kernel(
-    stream, cot, mask, unperm, w_hbm, to_hbm,
+    stream, cot, mask, unperm, order_hbm, w_hbm, to_hbm,
     up_out, grad_out,
-    w, wo, hat, qkv, back, mixed, dqkv, usend, urecv,
-    wsem, tosem, uss, urs,
+    w, wo, order, hat, qkv, back, mixed, probs, dqkv, usend, urecv, asend, arecv, msend, mrecv,
+    wsem, tosem, ordsem, uss, urs, mss, mrs,
 ):
     p = lax.axis_index("pos")
     f = lax.axis_index("frame")
+    par = lax.rem(p, 2)
+    mate = p + 1 - 2 * par
     barrier = pltpu.get_barrier_semaphore()
     greet(barrier, p, f, False, True)
+    pl.semaphore_signal(barrier, inc=1, device_id={"pos": mate})
+    order_copy = pltpu.make_async_copy(order_hbm, order, ordsem)
     to_copy = pltpu.make_async_copy(to_hbm, wo, tosem)
     to_copy.start()
     w_copies = [pltpu.make_async_copy(w_hbm.at[pl.ds(c * D, D)], w.at[c], wsem.at[c]) for c in range(3)]
     for c in w_copies:
         c.start()
+    order_copy.start()
     normed, inv = normalize(stream[...])
     hat[...] = normed
     normed = normed.astype(BF)
@@ -307,34 +328,49 @@
     for c in range(3):
         w_copies[c].wait()
         qkv[c] = dot(normed, w[c], 1, 1).astype(BF)
+    order_copy.wait()
+    for e in range(2):
+        asend[e] = dot(cot[...], order[e], 1, 0).astype(BF)
     mixed[...] = jnp.zeros_like(mixed)
     dqkv[...] = jnp.zeros_like(dqkv)
-    for h in range(HEADS):
+
+    def window(h):
         off = (h * HD) % 128
         start = h * HD - off
         width = 128 if off + HD <= 128 else 256
-        win = slice(start, start + width)
         lane = lax.broadcasted_iota(jnp.int32, (1, width), 1)
         keep = ((lane >= off) & (lane < off + HD)).astype(F32).astype(BF)
-        q, k, v, b = qkv[0, :, win], qkv[1, :, win], qkv[2, :, win], back[:, win]
-        qm, km, vm, bm = q * keep, k * keep, v * keep, b * keep
-        s = dot(qm, k, 1, 1) * SCALE + mask[...]
+        return slice(start, start + width), keep
+
+    for h in range(HEADS):
+        win, keep = window(h)
+        s = dot(qkv[0, :, win] * keep, qkv[1, :, win], 1, 1) * SCALE + mask[...]
         e = jnp.exp(s - jnp.max(s, axis=1, keepdims=True))
         prob = e * (1.0 / jnp.sum(e, axis=1, keepdims=True))
-        pb = prob.astype(BF)
-        mixed[:, win] += dot(pb, vm, 1, 0)
-        gp = dot(bm, v, 1, 1)
+        probs[h] = prob
+        mixed[:, win] += dot(prob.astype(BF), qkv[2, :, win] * keep, 1, 0)
+    msend[...] = mixed[...].astype(BF)
+    pl.semaphore_wait(barrier, NF)
+    a_copy = send(asend.at[1 - par], arecv, mss.at[0], mrs.at[0], "pos", mate)
+    m_copy = send(msend, mrecv, mss.at[1], mrs.at[1], "pos", mate)
+    a_copy.start()
+    m_copy.start()
+    for h in range(HEADS):
+        win, keep = window(h)
+        k, q = qkv[1, :, win] * keep, qkv[0, :, win] * keep
+        b = back[:, win] * keep
+        prob = probs[h]
+        gp = dot(b, qkv[2, :, win], 1, 1)
         gs = prob * (gp - jnp.sum(prob * gp, axis=1, keepdims=True)) * SCALE
         gs = gs.astype(BF)
-        dqkv[0, :, win] += dot(gs, km, 1, 0)
-        dqkv[1, :, win] += dot(gs, qm, 0, 0)
-        dqkv[2, :, win] += dot(pb, bm, 0, 0)
+        dqkv[0, :, win] += dot(gs, k, 1, 0)
+        dqkv[1, :, win] += dot(gs, q, 0, 0)
+        dqkv[2, :, win] += dot(prob.astype(BF), b, 0, 0)
     grad_hat = dot(dqkv[0].astype(BF), w[0], 1, 0)
     for c in range(1, 3):
         grad_hat += dot(dqkv[c].astype(BF), w[c], 1, 0)
     up = cot[...].astype(F32) + norm_back(grad_hat, hat[...], inv)
     usend[...] = up.astype(BF).reshape(NF, SLAB, D)
-    pl.semaphore_wait(barrier, NF - 1)
 
     def u_copy(s):
         to = lax.rem(f + s, NF)
@@ -345,9 +381,13 @@
         u_copy(s).start()
 
     urecv[pl.ds(f, 1)] = usend[pl.ds(f, 1)]
-    mb = mixed[...].astype(BF)
-    for r in range(0, D, 128):
-        grad_out[r : r + 128] = dot(cot[:, r : r + 128], mb, 0, 0).astype(BF)
+    a_copy.wait()
+    m_copy.wait()
+    mine = asend.at[par]
+    for r in range(0, GH, 128):
+        part = dot(mine[:, r : r + 128], msend[...], 0, 0)
+        part += dot(arecv[:, r : r + 128], mrecv[...], 0, 0)
+        grad_out[r : r + 128] = part.astype(BF)
 
     @pl.loop(1, NF)
     def _(s):
@@ -356,36 +396,43 @@
     up_out[...] = dot(unperm[...], urecv[...].reshape(TT, D), 1, 0).astype(BF)
 
 
-def time_block(stream, cot, mask, unperm, w, wo):
+def time_block(stream, cot, mask, unperm, order, w, wo):
     V = pltpu.VMEM
     sds = jax.ShapeDtypeStruct
     return pl.pallas_call(
         time_kernel,
-        out_shape=(sds((TOK, D), BF), sds((D, D), BF)),
-        in_specs=[vmem(), vmem(), vmem(), vmem(), anywhere(), anywhere()],
+        out_shape=(sds((TOK, D), BF), sds((GH, D), BF)),
+        in_specs=[vmem(), vmem(), vmem(), vmem(), anywhere(), anywhere(), anywhere()],
         out_specs=(vmem(), vmem()),
         scratch_shapes=[
-            V((3, D, D), BF), V((D, D), BF), V((TT, D), F32), V((3, TT, D), BF), V((TT, D), BF),
-            V((TT, D), F32), V((3, TT, D), F32), V((NF, SLAB, D), BF), V((NF, SLAB, D), BF),
-            DMA((3,)), DMA, DMA((NF,)), DMA((NF,)),
+            V((3, D, D), BF), V((D, D), BF), V((2, D, GH), BF), V((TT, D), F32), V((3, TT, D), BF),
+            V((TT, D), BF), V((TT, D), F32), V((HEADS, TT, TT), F32), V((3, TT, D), F32),
+            V((NF, SLAB, D), BF), V((NF, SLAB, D), BF),
+            V((2, TT, GH), BF), V((TT, GH), BF), V((TT, D), BF), V((TT, D), BF),
+            DMA((3,)), DMA, DMA, DMA((NF,)), DMA((NF,)), DMA((2,)), DMA((2,)),
         ],
         compiler_params=params(2),
-    )(stream, cot, mask, unperm, w, wo)
+    )(stream, cot, mask, unperm, order, w, wo)
 
 
 def space_backward_kernel(
-    x, up, mixed, spread, stat, att, qkv_hbm, gt_hbm, w_hbm, so_hbm,
-    grad_out, gs_out, gt_out,
-    w, so, qkv, bsend, brecv, gpart, grecv, hsend, hrecv, qbuf, kbuf, vbuf, kt, pbuf, sbuf,
-    dq, dk, dv, rsend, rrecv,
-    wsem, sosem, qsem, gsem, bss, brs, gss, grs, hss, hrs, rss, rrs,
+    x, up, mixed, spread, stat, att, order_hbm, qkv_hbm, gt_hbm, w_hbm, so_hbm,
+    grad_out, sums_out,
+    w, so, order, qkv, bsend, brecv, gpart, grecv, hsend, hrecv, asend, arecv, mrecv,
+    qbuf, kbuf, vbuf, bbuf, kt, pbuf, sbuf, dq, dk, dv, rsend, rrecv,
+    wsem, sosem, ordsem, qsem, gsem, bss, brs, gss, grs, hss, hrs, rss, rrs, mss, mrs,
 ):
     p = lax.axis_index("pos")
     f = lax.axis_index("frame")
     barrier = pltpu.get_barrier_semaphore()
+    par = lax.rem(p, 2)
+    chip = p // 2
+    mate = p + 1 - 2 * par
     greet(barrier, p, f, True, True)
     so_copy = pltpu.make_async_copy(so_hbm, so, sosem)
     so_copy.start()
+    order_copy = pltpu.make_async_copy(order_hbm, order, ordsem)
+    order_copy.start()
     qkv_copy = pltpu.make_async_copy(qkv_hbm, qkv, qsem)
     qkv_copy.start()
     gt_copy = pltpu.make_async_copy(gt_hbm, gpart.at[0], gsem)
@@ -394,10 +441,9 @@
     w_copy.start()
     so_copy.wait()
     back = dot(up[...], so[...], 1, 0)
-    pad = jnp.zeros((TOK, 128 - HD), F32)
+    back = back.reshape(FR, 3, GRP, D)
     for h in range(HEADS):
-        val = jnp.concatenate([back[:, h * HD : (h + 1) * HD], pad], axis=1).astype(BF)
-        bsend[:, h] = val.reshape(FR, PL, 128)
+        bsend[:, h] = pack([lanes(back[:, g], h) for g in range(3)])
     pl.semaphore_wait(barrier, NP - 1 + NF - 1)
 
     def b_copy(fr, s):
@@ -414,24 +460,36 @@
 
     def g_copy(g, s):
         to = lax.rem(f + s, NF)
-        rows = pl.ds(pl.multiple_of(to * GR, 16), GR)
+        rows = pl.ds(pl.multiple_of(to * GS, 16), GS)
         return send(gpart.at[g, rows], grecv.at[g, f], gss.at[g, s], grs.at[g, s], "frame", to)
 
+    m_copy = send(mixed, mrecv, mss.at[1], mrs.at[1], "pos", mate)
+    m_copy.start()
     gt_copy.wait()
 
     @pl.loop(1, NF)
     def _(s):
         g_copy(0, s).start()
 
-    for r in range(0, D, 128):
-        gpart[1, r : r + 128] = dot(up[:, r : r + 128], mixed[...], 0, 0).astype(BF)
+    order_copy.wait()
+    for e in range(2):
+        asend[e] = dot(up[...], order[e], 1, 0).astype(BF)
+    a_copy = send(asend.at[1 - par], arecv, mss.at[0], mrs.at[0], "pos", mate)
+    a_copy.start()
+    a_copy.wait()
+    m_copy.wait()
+    mine = asend.at[par]
+    for r in range(0, GH, 128):
+        part = dot(mine[:, r : r + 128], mixed[...], 0, 0)
+        part += dot(arecv[:, r : r + 128], mrecv[...], 0, 0)
+        gpart[1, r : r + 128] = part.astype(BF)
 
     @pl.loop(1, NF)
     def _(s):
         g_copy(1, s).start()
 
     for g in range(2):
-        grecv[g, pl.ds(f, 1)] = gpart[g, pl.ds(pl.multiple_of(f * GR, 16), GR)][None]
+        grecv[g, pl.ds(f, 1)] = gpart[g, pl.ds(pl.multiple_of(f * GS, 16), GS)][None]
 
     def r_copy(fr, s):
         to = lax.rem(p + s, NP)
@@ -455,11 +513,16 @@
         def _(s):
             b_copy(fr, s).wait_recv()
 
+        got = brecv[fr]
+        zeros = jnp.zeros((NP, GRP, 128 - HD), BF)
+        for g in range(3):
+            bbuf[:, g * GRP : (g + 1) * GRP] = jnp.concatenate([lanes(got, g), zeros], axis=-1)
+
         @pl.loop(0, ALL // BT)
         def _(t):
             at = pl.ds(pl.multiple_of(t * BT, BT), BT)
             q = qbuf[at]
-            b = brecv.reshape(FR, ALL, 128)[fr, at]
+            b = bbuf.reshape(ALL, 128)[at]
             total = jnp.sum(b.astype(F32).T * att[fr, :, at], axis=0, keepdims=True)
             lse = stat[fr, 0:1, at]
             for k in range(0, ALL, KC):
@@ -490,8 +553,10 @@
         rrecv[fr, pl.ds(p, 1)] = rsend[fr, pl.ds(p, 1)]
 
     def h_copy(g, s):
-        to = lax.rem(p + s, NP)
-        return send(hsend.at[g, to], hrecv.at[g, p], hss.at[g, s], hrs.at[g, s], "pos", to)
+        to = lax.rem(chip + s, NK)
+        return send(
+            hsend.at[g, to], hrecv.at[g, chip], hss.at[g, s], hrs.at[g, s], "pos", 2 * to + par
+        )
 
     for g in range(2):
 
@@ -502,13 +567,13 @@
         total = grecv[g, 0].astype(F32)
         for s in range(1, NF):
             total += grecv[g, s].astype(F32)
-        hsend[g] = dot(spread[...], total.astype(BF), 1, 0).astype(BF).reshape(NP, 16, D)
-
-        @pl.loop(1, NP)
+        hsend[g] = dot(spread[...], total.astype(BF), 1, 0).astype(BF).reshape(NK, 16, D)
+
+        @pl.loop(1, NK)
         def _(s):
             h_copy(g, s).start()
 
-        hrecv[g, pl.ds(p, 1)] = hsend[g, pl.ds(p, 1)]
+        hrecv[g, pl.ds(chip, 1)] = hsend[g, pl.ds(chip, 1)]
 
     w_copy.wait()
     for fr in range(FR):
@@ -526,52 +591,76 @@
         normed, inv = normalize(x[here])
         grad_out[here] = (up[here].astype(F32) + norm_back(grad_hat, normed, inv)).astype(BF)
 
-    for g, out in ((0, gt_out), (1, gs_out)):
-
-        @pl.loop(1, NP)
+    for g in range(2):
+
+        @pl.loop(1, NK)
         def _(s):
             h_copy(g, s).wait_recv()
 
         total = hrecv[g, 0].astype(F32)
-        for s in range(1, NP):
+        for s in range(1, NK):
             total += hrecv[g, s].astype(F32)
-        out[...] = total
+        sums_out[g] = total
 
     @pl.loop(1, NP)
     def _(s):
         for fr in range(FR):
             b_copy(fr, s).wait_send()
             r_copy(fr, s).wait_send()
+
+    @pl.loop(1, NF)
+    def _(s):
+        for g in range(2):
+            g_copy(g, s).wait_send()
+
+    @pl.loop(1, NK)
+    def _(s):
         for g in range(2):
             h_copy(g, s).wait_send()
 
-    @pl.loop(1, NF)
-    def _(s):
-        for g in range(2):
-            g_copy(g, s).wait_send()
-
-
-def space_backward(x, up, mixed, spread, stat, att, qkv, gt, w, so):
+
+def space_backward(x, up, mixed, spread, stat, att, order, qkv, gt, w, so):
     V = pltpu.VMEM
     sds = jax.ShapeDtypeStruct
     return pl.pallas_call(
         space_backward_kernel,
-        out_shape=(sds((TOK, D), BF), sds((16, D), F32), sds((16, D), F32)),
-        in_specs=[vmem()] * 6 + [anywhere()] * 4,
-        out_specs=(vmem(), vmem(), vmem()),
+        out_shape=(sds((TOK, D), BF), sds((2, 16, D), F32)),
+        in_specs=[vmem()] * 6 + [anywhere()] * 5,
+        out_specs=(vmem(), vmem()),
         scratch_shapes=[
-            V((3 * D, D), BF), V((D, D), BF), V((FR, NP, PL, 256), BF),
-            V((FR, NP, PL, 128), BF), V((FR, NP, PL, 128), BF),
-            V((2, D, D), BF), V((2, NF, GR, D), BF), V((2, NP, 16, D), BF), V((2, NP, 16, D), BF),
-            V((ALL, 128), BF), V((ALL, 128), BF), V((ALL, 128), BF), V((128, ALL), BF),
+            V((3 * D, D), BF), V((D, D), BF), V((2, D, GH), BF), V((FR, NP, PL, 256), BF),
+            V((FR, NP, GRP, 256), BF), V((FR, NP, GRP, 256), BF),
+            V((2, GH, D), BF), V((2, NF, GS, D), BF), V((2, NK, 16, D), BF), V((2, NK, 16, D), BF),
+            V((2, TOK, GH), BF), V((TOK, GH), BF), V((TOK, D), BF),
+            V((ALL, 128), BF), V((ALL, 128), BF), V((ALL, 128), BF), V((NP, PL, 128), BF),
+            V((128, ALL), BF),
             V((ALL, BT), BF), V((ALL, BT), BF),
             V((ALL, 128), F32), V((ALL, 128), F32), V((ALL, 128), F32),
             V((FR, NP, PL, 256), BF), V((FR, NP, PL, 256), BF),
-            DMA, DMA, DMA, DMA, DMA((FR, NP)), DMA((FR, NP)), DMA((2, NF)), DMA((2, NF)),
-            DMA((2, NP)), DMA((2, NP)), DMA((FR, NP)), DMA((FR, NP)),
+            DMA, DMA, DMA, DMA, DMA, DMA((FR, NP)), DMA((FR, NP)), DMA((2, NF)), DMA((2, NF)),
+            DMA((2, NK)), DMA((2, NK)), DMA((FR, NP)), DMA((FR, NP)), DMA((2,)), DMA((2,)),
         ],
         compiler_params=params(3),
-    )(x, up, mixed, spread, stat, att, qkv, gt, w, so)
+    )(x, up, mixed, spread, stat, att, order, qkv, gt, w, so)
+
+
+def finish_kernel(grad, sums, grad_out, gs_out, gt_out, sem):
+    copy = pltpu.make_async_copy(grad, grad_out, sem)
+    copy.start()
+    gt_out[...] = sums[0, :GR]
+    gs_out[...] = sums[1, :GR]
+    copy.wait()
+
+
+def finish(grad, sums):
+    sds = jax.ShapeDtypeStruct
+    return pl.pallas_call(
+        finish_kernel,
+        out_shape=(sds((TOK, D), BF), sds((GR, D), F32), sds((GR, D), F32)),
+        in_specs=[anywhere(), vmem()],
+        out_specs=(anywhere(), vmem(), vmem()),
+        scratch_shapes=[DMA],
+    )(grad, sums)
 
 
 def tables():
@@ -582,26 +671,31 @@
     perm = (real[:, None] & (col[:, None] == np.arange(TOK)[None])).astype(np.float32)
     place = np.where(real, inner % TP, -1)
     mask = np.where(place[:, None] == place[None], 0.0, -1e30).astype(np.float32)
-    row = np.arange(NP * 16)
-    spread = (row % 16 < GR // NP)[:, None] & (
-        ((row // 16) * (GR // NP) + row % 16)[:, None] == np.arange(GR)[None]
-    )
-    return jnp.asarray(perm, BF), jnp.asarray(perm.T, BF), jnp.asarray(mask), jnp.asarray(spread, BF)
+    row = np.arange(NK * 16)
+    spread = (row % 16 < GR)[:, None] & (((row // 16) * GR + row % 16)[:, None] == np.arange(GS)[None])
+    col = np.arange(2 * GH)
+    core, slab, inner = col // GH, col % GH // GS, col % GS
+    source = (slab * NP + 2 * (inner // GR) + core) * GR + inner % GR
+    order = (inner < NK * GR)[None] & (np.arange(D)[:, None] == source[None])
+    order = order.reshape(D, 2, GH).transpose(1, 0, 2)
+    return [jnp.asarray(t.astype(np.float32), BF) for t in (perm, perm.T, spread, order)] + [
+        jnp.asarray(mask)
+    ]
 
 
 def shards(inputs, cotangent, space_projection, space_output, time_projection, time_output):
-    perm, unperm, mask, spread = tables()
+    perm, unperm, spread, order, mask = tables()
     x = inputs.reshape(TOK, D)
     cot = cotangent.reshape(TOK, D)
     qkv, stat, att, mixed, stream_t, cot_t = space_forward(x, cot, perm, space_projection, space_output)
     up, gt = time_block(
-        stream_t.reshape(TT, D), cot_t.reshape(TT, D), mask, unperm, time_projection, time_output
+        stream_t.reshape(TT, D), cot_t.reshape(TT, D), mask, unperm, order, time_projection, time_output
     )
-    grad, gs, gt = space_backward(
-        x, up, mixed, spread, stat, att, qkv, gt, space_projection, space_output
+    grad, sums = space_backward(
+        x, up, mixed, spread, stat, att, order, qkv, gt, space_projection, space_output
     )
-    rows = GR // NP
-    return grad.reshape(FR, PL, D), gs[:rows], gt[:rows]
+    grad, gs, gt = finish(grad, sums)
+    return grad.reshape(FR, PL, D), gs, gt
 
 
 def solution(mesh):

time: 220 us -> 183 us (0.83)
  the two profiles are of different devices: /device:TPU:1 before, /device:TPU:124 now
where the time goes in v3:
time: 183 us; the launch traced here: 182 us
  Pallas kernels  182 us (99%)
    pallas_call x1, Pallas kernels, space_backward(): pl.pallas_call(space_backward_kernel, out_shape=(sds((TOK, D), BF), sds((...  79.8 us
    pallas_call x1, Pallas kernels, space_forward(): pl.pallas_call(space_forward_kernel, out_shape=(sds((FR, NP, PL, 256), BF...  54.9 us
    pallas_call x1, Pallas kernels, time_block(): pl.pallas_call(time_kernel, out_shape=(sds((TOK, D), BF), sds((GH, D), BF...  30.8 us
    pallas_call x1, Pallas kernels, finish(): pl.pallas_call(finish_kernel, out_shape=(sds((TOK, D), BF), sds((GR, D),...  16.1 us

profile of v3, /device:TPU:124, one launch (start us, length us, event | category | flops | bytes accessed | tf_op | source)
XLA Modules:
  0.0 182.4 jit_solution(11487986444721943071)
XLA Ops:
  0.6 54.9 %shard_map.130 = (bf16[2,16,96,256]{3,2,1,0:T(8,128)(2,1)}, f32[2,8,1536]{2,1,0:T(8,128)}, f32[2,128,1536]{2,1,0:T(8,128)}, bf16[192,1152]{1,0:T(8,128)(2,1)}, b...) custom-call(bf16[192,1152]{1,0:T(8,128)(2,1)} %bitcast.5, bf16[192,1152]{1,0:T(8,128)(2,1)} %bitcast.9, ...), custom_call_target="tpu_custom_call" | custom-call | tf_op jit(solution)/shard_map/pallas_call | solution.py:278
  55.5 30.8 %shard_map.131 = (bf16[192,1152]{1,0:T(8,128)(2,1)}, bf16[640,1152]{1,0:T(8,128)(2,1)}) custom-call(bf16[256,1152]{1,0:T(8,128)(2,1)} %bitcast.7, bf16[256,1152]{1,0:T(8,128)(2,1)} %bitcast.8, f32[256,256]{1,0:T(8,128)} %constant.14.clone.mask, bf16[192,256]{1,0:T(8,128)(2,1)} %constant.11.clone.unperm, bf16[2,1152,640]{2,1,0:T(8,128)(2,1)} %constant.13.clone.order_hbm, ...), custom_call_target="tpu_custom_call" | custom-call | tf_op jit(solution)/shard_map/pallas_call | solution.py:402
  86.3 79.8 %shard_map.132 = (bf16[192,1152]{1,0:T(8,128)(2,1)}, f32[2,16,1152]{2,1,0:T(8,128)}) custom-call(bf16[192,1152]{1,0:T(8,128)(2,1)} %bitcast.6, bf16[192,1152]{1,0:T(8,128)(2,1)} %get-tuple-element.18.up, bf16[192,1152]{1,0:T(8,128)(2,1)} %get-tuple-element.19.mixed, bf16[128,80]{1,0:T(8,128)(2,1)} %constant.12.clone.spread, ...), custom_call_target="tpu_custom_call" | custom-call | tf_op jit(solution)/shard_map/pallas_call | solution.py:625
  166.1 16.1 %shard_map.133 = (bf16[192,1152]{1,0:T(8,128)(2,1)}, f32[9,1152]{1,0:T(8,128)}, f32[9,1152]{1,0:T(8,128)}) custom-call(bf16[192,1152]{1,0:T(8,128)(2,1)} %get-tuple-element.24.grad, f32[2,16,1152]{2,1,0:T(8,128)} %get-tuple-element.25.sums), custom_call_target="tpu_custom_call" | custom-call | tf_op jit(solution)/shard_map/pallas_call | solution.py:657

commit v4 on v3

--- a/solution.py
+++ b/solution.py
@@ -51,6 +51,12 @@
     return inv_std * (grad_hat - mean_grad - normed * mean_proj)
 
 
+def pos_peer(p, s, sign):
+    v = 7 - (s // 2 + 7) % 8
+    x, z = lax.rem(p // 8 + v // 4, 2), lax.rem(lax.rem(p // 2, 4) + sign * (v % 4) + 4, 4)
+    return 8 * x + 2 * z + lax.rem(lax.rem(p, 2) + s % 2, 2)
+
+
 def pack(parts):
     shape = parts[0].shape[:-1] + (256 - 3 * HD,)
     return jnp.concatenate(list(parts) + [jnp.zeros(shape, F32)], axis=-1).astype(BF)
@@ -89,12 +95,11 @@
     p = lax.axis_index("pos")
     f = lax.axis_index("frame")
     par = lax.rem(p, 2)
-    half = p // 2
     barrier = pltpu.get_barrier_semaphore()
     greet(barrier, p, f, True, True)
 
     def w_copy(i, c):
-        pair = lax.rem(half + i, 8)
+        pair = pos_peer(p, 2 * i, 1) // 2
         rows = pl.ds(pl.multiple_of(c * D + pair * 144, 16), 144)
         return pltpu.make_async_copy(w_hbm.at[rows], w.at[i, pl.ds(c * 144, 144)], wsem.at[i, c])
 
@@ -106,12 +111,8 @@
     hat[...] = normalize(x[...])[0].astype(BF)
     pl.semaphore_wait(barrier, NP - 1 + NF - 1)
 
-    def peer(s, sign):
-        pair = lax.rem(half + sign * (s // 2) + 8, 8)
-        return 2 * pair + lax.rem(par + s, 2)
-
     def q_copy(fr, s):
-        return send(qsend.at[s, fr], qkv.at[fr, p], qss.at[fr, s], qrs.at[fr, s], "pos", peer(s, 1))
+        return send(qsend.at[s, fr], qkv.at[fr, p], qss.at[fr, s], qrs.at[fr, s], "pos", pos_peer(p, s, 1))
 
     @pl.loop(0, 8)
     def _(i):
@@ -300,38 +301,49 @@
     )(x, cot, perm, w, so)
 
 
-def time_kernel(
-    stream, cot, mask, unperm, order_hbm, w_hbm, to_hbm,
-    up_out, grad_out,
-    w, wo, order, hat, qkv, back, mixed, probs, dqkv, usend, urecv, asend, arecv, msend, mrecv,
-    wsem, tosem, ordsem, uss, urs, mss, mrs,
+def rest_kernel(
+    stream, cot, mask, unperm, spread, x, mixed, stat, att,
+    order_hbm, tw_hbm, to_hbm, qkv_hbm, w_hbm, so_hbm,
+    grad_out, sums_out,
+    w, wo, so, order, hat, tqkv, back, tmixed, probs, dqkv, usend, urecv, up,
+    tasend, tarecv, tmsend, tmrecv, asend, arecv, mrecv,
+    qkv, bsend, brecv, gpart, grecv, hsend, hrecv,
+    qbuf, kbuf, vbuf, bbuf, kt, pbuf, sbuf, dq, dk, dv, rsend, rrecv,
+    wsem, tosem, sosem, ordsem, qsem, uss, urs, mss, mrs, bss, brs, gss, grs, hss, hrs, rss, rrs,
 ):
     p = lax.axis_index("pos")
     f = lax.axis_index("frame")
     par = lax.rem(p, 2)
+    chip = p // 2
     mate = p + 1 - 2 * par
     barrier = pltpu.get_barrier_semaphore()
-    greet(barrier, p, f, False, True)
-    pl.semaphore_signal(barrier, inc=1, device_id={"pos": mate})
-    order_copy = pltpu.make_async_copy(order_hbm, order, ordsem)
+    greet(barrier, p, f, True, True)
     to_copy = pltpu.make_async_copy(to_hbm, wo, tosem)
     to_copy.start()
-    w_copies = [pltpu.make_async_copy(w_hbm.at[pl.ds(c * D, D)], w.at[c], wsem.at[c]) for c in range(3)]
-    for c in w_copies:
+    tw_copies = [
+        pltpu.make_async_copy(tw_hbm.at[pl.ds(c * D, D)], w.at[c], wsem.at[c]) for c in range(3)
+    ]
+    for c in tw_copies:
         c.start()
+    order_copy = pltpu.make_async_copy(order_hbm, order, ordsem)
     order_copy.start()
+    so_copy = pltpu.make_async_copy(so_hbm, so, sosem)
+    so_copy.start()
+    qkv_copy = pltpu.make_async_copy(qkv_hbm, qkv, qsem)
+    qkv_copy.start()
+
     normed, inv = normalize(stream[...])
     hat[...] = normed
     normed = normed.astype(BF)
     to_copy.wait()
     back[...] = dot(cot[...], wo[...], 1, 0).astype(BF)
     for c in range(3):
-        w_copies[c].wait()
-        qkv[c] = dot(normed, w[c], 1, 1).astype(BF)
+        tw_copies[c].wait()
+        tqkv[c] = dot(normed, w[c], 1, 1).astype(BF)
     order_copy.wait()
     for e in range(2):
-        asend[e] = dot(cot[...], order[e], 1, 0).astype(BF)
-    mixed[...] = jnp.zeros_like(mixed)
+        tasend[e] = dot(cot[...], order[e], 1, 0).astype(BF)
+    tmixed[...] = jnp.zeros_like(tmixed)
     dqkv[...] = jnp.zeros_like(dqkv)
 
     def window(h):
@@ -344,23 +356,25 @@
 
     for h in range(HEADS):
         win, keep = window(h)
-        s = dot(qkv[0, :, win] * keep, qkv[1, :, win], 1, 1) * SCALE + mask[...]
+        s = dot(tqkv[0, :, win] * keep, tqkv[1, :, win], 1, 1) * SCALE + mask[...]
         e = jnp.exp(s - jnp.max(s, axis=1, keepdims=True))
         prob = e * (1.0 / jnp.sum(e, axis=1, keepdims=True))
         probs[h] = prob
-        mixed[:, win] += dot(prob.astype(BF), qkv[2, :, win] * keep, 1, 0)
-    msend[...] = mixed[...].astype(BF)
-    pl.semaphore_wait(barrier, NF)
-    a_copy = send(asend.at[1 - par], arecv, mss.at[0], mrs.at[0], "pos", mate)
-    m_copy = send(msend, mrecv, mss.at[1], mrs.at[1], "pos", mate)
-    a_copy.start()
+        tmixed[:, win] += dot(prob.astype(BF), tqkv[2, :, win] * keep, 1, 0)
+    tmsend[...] = tmixed[...].astype(BF)
+    pl.semaphore_wait(barrier, NP - 1 + NF - 1)
+    ta_copy = send(tasend.at[1 - par], tarecv, mss.at[0], mrs.at[0], "pos", mate)
+    tm_copy = send(tmsend, tmrecv, mss.at[1], mrs.at[1], "pos", mate)
+    m_copy = send(mixed, mrecv, mss.at[2], mrs.at[2], "pos", mate)
+    ta_copy.start()
+    tm_copy.start()
     m_copy.start()
     for h in range(HEADS):
         win, keep = window(h)
-        k, q = qkv[1, :, win] * keep, qkv[0, :, win] * keep
+        k, q = tqkv[1, :, win] * keep, tqkv[0, :, win] * keep
         b = back[:, win] * keep
         prob = probs[h]
-        gp = dot(b, qkv[2, :, win], 1, 1)
+        gp = dot(b, tqkv[2, :, win], 1, 1)
         gs = prob * (gp - jnp.sum(prob * gp, axis=1, keepdims=True)) * SCALE
         gs = gs.astype(BF)
         dqkv[0, :, win] += dot(gs, k, 1, 0)
@@ -369,8 +383,8 @@
     grad_hat = dot(dqkv[0].astype(BF), w[0], 1, 0)
     for c in range(1, 3):
         grad_hat += dot(dqkv[c].astype(BF), w[c], 1, 0)
-    up = cot[...].astype(F32) + norm_back(grad_hat, hat[...], inv)
-    usend[...] = up.astype(BF).reshape(NF, SLAB, D)
+    turned = cot[...].astype(F32) + norm_back(grad_hat, hat[...], inv)
+    usend[...] = turned.astype(BF).reshape(NF, SLAB, D)
 
     def u_copy(s):
         to = lax.rem(f + s, NF)
@@ -381,131 +395,87 @@
         u_copy(s).start()
 
     urecv[pl.ds(f, 1)] = usend[pl.ds(f, 1)]
-    a_copy.wait()
-    m_copy.wait()
-    mine = asend.at[par]
-    for r in range(0, GH, 128):
-        part = dot(mine[:, r : r + 128], msend[...], 0, 0)
-        part += dot(arecv[:, r : r + 128], mrecv[...], 0, 0)
-        grad_out[r : r + 128] = part.astype(BF)
-
-    @pl.loop(1, NF)
-    def _(s):
-        u_copy(s).wait()
-
-    up_out[...] = dot(unperm[...], urecv[...].reshape(TT, D), 1, 0).astype(BF)
-
-
-def time_block(stream, cot, mask, unperm, order, w, wo):
-    V = pltpu.VMEM
-    sds = jax.ShapeDtypeStruct
-    return pl.pallas_call(
-        time_kernel,
-        out_shape=(sds((TOK, D), BF), sds((GH, D), BF)),
-        in_specs=[vmem(), vmem(), vmem(), vmem(), anywhere(), anywhere(), anywhere()],
-        out_specs=(vmem(), vmem()),
-        scratch_shapes=[
-            V((3, D, D), BF), V((D, D), BF), V((2, D, GH), BF), V((TT, D), F32), V((3, TT, D), BF),
-            V((TT, D), BF), V((TT, D), F32), V((HEADS, TT, TT), F32), V((3, TT, D), F32),
-            V((NF, SLAB, D), BF), V((NF, SLAB, D), BF),
-            V((2, TT, GH), BF), V((TT, GH), BF), V((TT, D), BF), V((TT, D), BF),
-            DMA((3,)), DMA, DMA, DMA((NF,)), DMA((NF,)), DMA((2,)), DMA((2,)),
-        ],
-        compiler_params=params(2),
-    )(stream, cot, mask, unperm, order, w, wo)
-
-
-def space_backward_kernel(
-    x, up, mixed, spread, stat, att, order_hbm, qkv_hbm, gt_hbm, w_hbm, so_hbm,
-    grad_out, sums_out,
-    w, so, order, qkv, bsend, brecv, gpart, grecv, hsend, hrecv, asend, arecv, mrecv,
-    qbuf, kbuf, vbuf, bbuf, kt, pbuf, sbuf, dq, dk, dv, rsend, rrecv,
-    wsem, sosem, ordsem, qsem, gsem, bss, brs, gss, grs, hss, hrs, rss, rrs, mss, mrs,
-):
-    p = lax.axis_index("pos")
-    f = lax.axis_index("frame")
-    barrier = pltpu.get_barrier_semaphore()
-    par = lax.rem(p, 2)
-    chip = p // 2
-    mate = p + 1 - 2 * par
-    greet(barrier, p, f, True, True)
-    so_copy = pltpu.make_async_copy(so_hbm, so, sosem)
-    so_copy.start()
-    order_copy = pltpu.make_async_copy(order_hbm, order, ordsem)
-    order_copy.start()
-    qkv_copy = pltpu.make_async_copy(qkv_hbm, qkv, qsem)
-    qkv_copy.start()
-    gt_copy = pltpu.make_async_copy(gt_hbm, gpart.at[0], gsem)
-    gt_copy.start()
-    w_copy = pltpu.make_async_copy(w_hbm, w, wsem)
-    w_copy.start()
-    so_copy.wait()
-    back = dot(up[...], so[...], 1, 0)
-    back = back.reshape(FR, 3, GRP, D)
-    for h in range(HEADS):
-        bsend[:, h] = pack([lanes(back[:, g], h) for g in range(3)])
-    pl.semaphore_wait(barrier, NP - 1 + NF - 1)
-
-    def b_copy(fr, s):
-        to = lax.rem(p + s, NP)
-        return send(bsend.at[fr, to], brecv.at[fr, p], bss.at[fr, s], brs.at[fr, s], "pos", to)
-
-    for fr in range(FR):
-
-        @pl.loop(1, NP)
-        def _(s):
-            b_copy(fr, s).start()
-
-    brecv[:, pl.ds(p, 1)] = bsend[:, pl.ds(p, 1)]
+
+    w_copies = [
+        pltpu.make_async_copy(w_hbm.at[pl.ds(c * D, D)], w.at[c], wsem.at[c]) for c in range(3)
+    ]
+    for c in w_copies:
+        c.start()
 
     def g_copy(g, s):
         to = lax.rem(f + s, NF)
         rows = pl.ds(pl.multiple_of(to * GS, 16), GS)
         return send(gpart.at[g, rows], grecv.at[g, f], gss.at[g, s], grs.at[g, s], "frame", to)
 
-    m_copy = send(mixed, mrecv, mss.at[1], mrs.at[1], "pos", mate)
-    m_copy.start()
-    gt_copy.wait()
-
-    @pl.loop(1, NF)
-    def _(s):
-        g_copy(0, s).start()
-
-    order_copy.wait()
+    def gradient(g, mine, left, theirs, right):
+        for r in range(0, GH, 128):
+            part = dot(mine[:, r : r + 128], left[...], 0, 0)
+            part += dot(theirs[:, r : r + 128], right[...], 0, 0)
+            gpart[g, r : r + 128] = part.astype(BF)
+
+        @pl.loop(1, NF)
+        def _(s):
+            g_copy(g, s).start()
+
+        grecv[g, pl.ds(f, 1)] = gpart[g, pl.ds(pl.multiple_of(f * GS, 16), GS)][None]
+
+    ta_copy.wait()
+    tm_copy.wait()
+    gradient(0, tasend.at[par], tmsend, tarecv, tmrecv)
+
+    qkv_copy.wait()
+    so_copy.wait()
+    lane = lax.broadcasted_iota(jnp.int32, (1, 128), 1)
+    keep = (lane < HD).astype(F32).astype(BF)
+    zeros = jnp.zeros((ALL, 128 - HD), BF)
+    for fr in range(FR):
+        rows = qkv[fr].reshape(ALL, 256)
+        qbuf[fr] = rows[:, :128] * keep
+        k = rows[:, HD : HD + 128] * keep
+        kbuf[fr] = k
+        kt[fr] = k.T
+        vbuf[fr] = jnp.concatenate([rows[:, 2 * HD : 3 * HD], zeros], axis=1)
+
+    @pl.loop(1, NF)
+    def _(s):
+        u_copy(s).wait_recv()
+
+    up[...] = dot(unperm[...], urecv[...].reshape(TT, D), 1, 0).astype(BF)
+
+    sback = dot(up[...], so[...], 1, 0).reshape(FR, 3, GRP, D)
+    for h in range(HEADS):
+        bsend[:, h] = pack([lanes(sback[:, g], h) for g in range(3)])
+
+    def b_copy(fr, s):
+        to, dst = pos_peer(p, s, 1), p
+        return send(bsend.at[fr, to], brecv.at[fr, dst], bss.at[fr, s], brs.at[fr, s], "pos", to)
+
+    for fr in range(FR):
+
+        @pl.loop(1, NP)
+        def _(s):
+            b_copy(fr, s).start()
+
+    brecv[:, pl.ds(p, 1)] = bsend[:, pl.ds(p, 1)]
     for e in range(2):
         asend[e] = dot(up[...], order[e], 1, 0).astype(BF)
-    a_copy = send(asend.at[1 - par], arecv, mss.at[0], mrs.at[0], "pos", mate)
+    a_copy = send(asend.at[1 - par], arecv, mss.at[3], mrs.at[3], "pos", mate)
     a_copy.start()
     a_copy.wait()
     m_copy.wait()
-    mine = asend.at[par]
-    for r in range(0, GH, 128):
-        part = dot(mine[:, r : r + 128], mixed[...], 0, 0)
-        part += dot(arecv[:, r : r + 128], mrecv[...], 0, 0)
-        gpart[1, r : r + 128] = part.astype(BF)
-
-    @pl.loop(1, NF)
-    def _(s):
-        g_copy(1, s).start()
-
-    for g in range(2):
-        grecv[g, pl.ds(f, 1)] = gpart[g, pl.ds(pl.multiple_of(f * GS, 16), GS)][None]
+    gradient(1, asend.at[par], mixed, arecv, mrecv)
 
     def r_copy(fr, s):
-        to = lax.rem(p + s, NP)
+        to = pos_peer(p, s, 1)
         return send(rsend.at[fr, to], rrecv.at[fr, p], rss.at[fr, s], rrs.at[fr, s], "pos", to)
 
-    qkv_copy.wait()
-    lane = lax.broadcasted_iota(jnp.int32, (1, 128), 1)
-    keep = (lane < HD).astype(F32).astype(BF)
+    def h_copy(g, s):
+        to = lax.rem(chip + s, NK)
+        return send(
+            hsend.at[g, to], hrecv.at[g, chip], hss.at[g, s], hrs.at[g, s], "pos", 2 * to + par
+        )
+
     for fr in range(FR):
-        rows = qkv[fr].reshape(ALL, 256)
-        zeros = jnp.zeros((ALL, 128 - HD), BF)
-        qbuf[...] = rows[:, :128] * keep
-        k = rows[:, HD : HD + 128] * keep
-        kbuf[...] = k
-        kt[...] = k.T
-        vbuf[...] = jnp.concatenate([rows[:, 2 * HD : 3 * HD], zeros], axis=1)
         dk[...] = jnp.zeros_like(dk)
         dv[...] = jnp.zeros_like(dv)
 
@@ -521,30 +491,22 @@
         @pl.loop(0, ALL // BT)
         def _(t):
             at = pl.ds(pl.multiple_of(t * BT, BT), BT)
-            q = qbuf[at]
+            q = qbuf[fr, at]
             b = bbuf.reshape(ALL, 128)[at]
             total = jnp.sum(b.astype(F32).T * att[fr, :, at], axis=0, keepdims=True)
             lse = stat[fr, 0:1, at]
             for k in range(0, ALL, KC):
-                s = dot(kbuf[k : k + KC], q, 1, 1)
-                gp = dot(vbuf[k : k + KC], b, 1, 1)
+                s = dot(kbuf[fr, k : k + KC], q, 1, 1)
+                gp = dot(vbuf[fr, k : k + KC], b, 1, 1)
                 prob = jnp.exp2(s * (SCALE * LOG2E) - lse)
                 pbuf[k : k + KC] = prob.astype(BF)
                 sbuf[k : k + KC] = (prob * (gp - total)).astype(BF)
             dv[...] += dot(pbuf[...], b, 1, 0)
             dk[...] += dot(sbuf[...], q, 1, 0)
-            dq[at] = dot(kt[...], sbuf[...], 1, 0).T
-
-        val = jnp.concatenate(
-            [
-                dq[:, :HD] * SCALE,
-                dk[:, :HD] * SCALE,
-                dv[:, :HD],
-                jnp.zeros((ALL, 256 - 3 * HD), F32),
-            ],
-            axis=1,
-        )
-        rsend[fr] = val.astype(BF).reshape(NP, PL, 256)
+            dq[at] = dot(kt[fr], sbuf[...], 1, 0).T
+
+        val = pack([dq[:, :HD] * SCALE, dk[:, :HD] * SCALE, dv[:, :HD]])
+        rsend[fr] = val.reshape(NP, PL, 256)
 
         @pl.loop(1, NP)
         def _(s):
@@ -552,14 +514,7 @@
 
         rrecv[fr, pl.ds(p, 1)] = rsend[fr, pl.ds(p, 1)]
 
-    def h_copy(g, s):
-        to = lax.rem(chip + s, NK)
-        return send(
-            hsend.at[g, to], hrecv.at[g, chip], hss.at[g, s], hrs.at[g, s], "pos", 2 * to + par
-        )
-
-    for g in range(2):
-
+    def spread_out(g):
         @pl.loop(1, NF)
         def _(s):
             g_copy(g, s).wait_recv()
@@ -575,9 +530,7 @@
 
         hrecv[g, pl.ds(chip, 1)] = hsend[g, pl.ds(chip, 1)]
 
-    w_copy.wait()
-    for fr in range(FR):
-
+    def finish_rows(fr):
         @pl.loop(1, NP)
         def _(s):
             r_copy(fr, s).wait_recv()
@@ -585,12 +538,18 @@
         got = [rrecv[fr, h].astype(F32) for h in range(HEADS)]
         grad_hat = jnp.zeros((PL, D), F32)
         for c in range(3):
-            part = jnp.concatenate([v[:, c * HD : (c + 1) * HD] for v in got], axis=1)
-            grad_hat += dot(part.astype(BF), w[c * D : (c + 1) * D], 1, 0)
+            part = jnp.concatenate([lanes(v, c) for v in got], axis=1)
+            grad_hat += dot(part.astype(BF), w[c], 1, 0)
         here = slice(fr * PL, (fr + 1) * PL)
         normed, inv = normalize(x[here])
         grad_out[here] = (up[here].astype(F32) + norm_back(grad_hat, normed, inv)).astype(BF)
 
+    spread_out(0)
+    for c in w_copies:
+        c.wait()
+    finish_rows(0)
+    spread_out(1)
+    finish_rows(1)
     for g in range(2):
 
         @pl.loop(1, NK)
@@ -610,6 +569,7 @@
 
     @pl.loop(1, NF)
     def _(s):
+        u_copy(s).wait_send()
         for g in range(2):
             g_copy(g, s).wait_send()
 
@@ -619,37 +579,39 @@
             h_copy(g, s).wait_send()
 
 
-def space_backward(x, up, mixed, spread, stat, att, order, qkv, gt, w, so):
+def rest(stream, cot, mask, unperm, spread, x, mixed, stat, att, order, tw, wo, qkv, w, so):
     V = pltpu.VMEM
     sds = jax.ShapeDtypeStruct
     return pl.pallas_call(
-        space_backward_kernel,
+        rest_kernel,
         out_shape=(sds((TOK, D), BF), sds((2, 16, D), F32)),
-        in_specs=[vmem()] * 6 + [anywhere()] * 5,
+        in_specs=[vmem()] * 9 + [anywhere()] * 6,
         out_specs=(vmem(), vmem()),
         scratch_shapes=[
-            V((3 * D, D), BF), V((D, D), BF), V((2, D, GH), BF), V((FR, NP, PL, 256), BF),
-            V((FR, NP, GRP, 256), BF), V((FR, NP, GRP, 256), BF),
+            V((3, D, D), BF), V((D, D), BF), V((D, D), BF), V((2, D, GH), BF), V((TT, D), F32),
+            V((3, TT, D), BF), V((TT, D), BF), V((TT, D), F32), V((HEADS, TT, TT), F32),
+            V((3, TT, D), F32), V((NF, SLAB, D), BF), V((NF, SLAB, D), BF), V((TOK, D), BF),
+            V((2, TT, GH), BF), V((TT, GH), BF), V((TT, D), BF), V((TT, D), BF),
+            V((2, TOK, GH), BF), V((TOK, GH), BF), V((TOK, D), BF),
+            V((FR, NP, PL, 256), BF), V((FR, NP, GRP, 256), BF), V((FR, NP, GRP, 256), BF),
             V((2, GH, D), BF), V((2, NF, GS, D), BF), V((2, NK, 16, D), BF), V((2, NK, 16, D), BF),
-            V((2, TOK, GH), BF), V((TOK, GH), BF), V((TOK, D), BF),
-            V((ALL, 128), BF), V((ALL, 128), BF), V((ALL, 128), BF), V((NP, PL, 128), BF),
-            V((128, ALL), BF),
+            V((FR, ALL, 128), BF), V((FR, ALL, 128), BF), V((FR, ALL, 128), BF),
+            V((NP, PL, 128), BF), V((FR, 128, ALL), BF),
             V((ALL, BT), BF), V((ALL, BT), BF),
             V((ALL, 128), F32), V((ALL, 128), F32), V((ALL, 128), F32),
             V((FR, NP, PL, 256), BF), V((FR, NP, PL, 256), BF),
-            DMA, DMA, DMA, DMA, DMA, DMA((FR, NP)), DMA((FR, NP)), DMA((2, NF)), DMA((2, NF)),
-            DMA((2, NK)), DMA((2, NK)), DMA((FR, NP)), DMA((FR, NP)), DMA((2,)), DMA((2,)),
+            DMA((3,)), DMA, DMA, DMA, DMA, DMA((NF,)), DMA((NF,)), DMA((4,)), DMA((4,)),
+            DMA((FR, NP)), DMA((FR, NP)), DMA((2, NF)), DMA((2, NF)),
+            DMA((2, NK)), DMA((2, NK)), DMA((FR, NP)), DMA((FR, NP)),
         ],
-        compiler_params=params(3),
-    )(x, up, mixed, spread, stat, att, order, qkv, gt, w, so)
-
-
-def finish_kernel(grad, sums, grad_out, gs_out, gt_out, sem):
-    copy = pltpu.make_async_copy(grad, grad_out, sem)
-    copy.start()
+        compiler_params=params(2),
+    )(stream, cot, mask, unperm, spread, x, mixed, stat, att, order, tw, wo, qkv, w, so)
+
+
+def finish_kernel(grad, sums, grad_out, gs_out, gt_out):
+    grad_out[...] = grad[...]
     gt_out[...] = sums[0, :GR]
     gs_out[...] = sums[1, :GR]
-    copy.wait()
 
 
 def finish(grad, sums):
@@ -657,9 +619,8 @@
     return pl.pallas_call(
         finish_kernel,
         out_shape=(sds((TOK, D), BF), sds((GR, D), F32), sds((GR, D), F32)),
-        in_specs=[anywhere(), vmem()],
-        out_specs=(anywhere(), vmem(), vmem()),
-        scratch_shapes=[DMA],
+        in_specs=[vmem(), vmem()],
+        out_specs=(vmem(), vmem(), vmem()),
     )(grad, sums)
 
 
@@ -688,11 +649,9 @@
     x = inputs.reshape(TOK, D)
     cot = cotangent.reshape(TOK, D)
     qkv, stat, att, mixed, stream_t, cot_t = space_forward(x, cot, perm, space_projection, space_output)
-    up, gt = time_block(
-        stream_t.reshape(TT, D), cot_t.reshape(TT, D), mask, unperm, order, time_projection, time_output
-    )
-    grad, sums = space_backward(
-        x, up, mixed, spread, stat, att, order, qkv, gt, space_projection, space_output
+    grad, sums = rest(
+        stream_t.reshape(TT, D), cot_t.reshape(TT, D), mask, unperm, spread, x, mixed, stat, att,
+        order, time_projection, time_output, qkv, space_projection, space_output,
     )
     grad, gs, gt = finish(grad, sums)
     return grad.reshape(FR, PL, D), gs, gt

time: 183 us -> 159 us (0.87)
  the two profiles are of different devices: /device:TPU:124 before, /device:TPU:24 now
where the time goes in v4:
time: 159 us
  Pallas kernels  158 us (99%)
    pallas_call x1, Pallas kernels, rest(): pl.pallas_call(rest_kernel, out_shape=(sds((TOK, D), BF), sds((2, 16, D),...  100 us
    pallas_call x1, Pallas kernels, space_forward(): pl.pallas_call(space_forward_kernel, out_shape=(sds((FR, NP, PL, 256), BF...  56.1 us

profile of v4, /device:TPU:24, one launch (start us, length us, event | category | flops | bytes accessed | tf_op | source)
XLA Modules:
  0.0 158.6 jit_solution(6941187805641601177)
XLA Ops:
  0.6 56.1 %shard_map.130 = (bf16[2,16,96,256]{3,2,1,0:T(8,128)(2,1)}, f32[2,8,1536]{2,1,0:T(8,128)}, f32[2,128,1536]{2,1,0:T(8,128)}, bf16[192,1152]{1,0:T(8,128)(2,1)}, b...) custom-call(bf16[192,1152]{1,0:T(8,128)(2,1)} %bitcast.5, bf16[192,1152]{1,0:T(8,128)(2,1)} %bitcast.9, ...), custom_call_target="tpu_custom_call" | custom-call | tf_op jit(solution)/shard_map/pallas_call | solution.py:279
  56.8 100.0 %shard_map.131 = (bf16[192,1152]{1,0:T(8,128)(2,1)}, f32[2,16,1152]{2,1,0:T(8,128)}) custom-call(bf16[256,1152]{1,0:T(8,128)(2,1)} %bitcast.7, bf16[256,1152]{1,0:T(8,128)(2,1)} %bitcast.8, f32[256,256]{1,0:T(8,128)} %constant.14.clone.mask, bf16[192,256]{1,0:T(8,128)(2,1)} %constant.11.clone.unperm, bf16[128,80]{1,0:T(8,128)(2,1)} %constant.12.clone.spread, ...), custom_call_target="tpu_custom_call" | custom-call | tf_op jit(solution)/shard_map/pallas_call | solution.py:585
  156.7 1.9 %shard_map.132 = (bf16[192,1152]{1,0:T(8,128)(2,1)}, f32[9,1152]{1,0:T(8,128)}, f32[9,1152]{1,0:T(8,128)}) custom-call(bf16[192,1152]{1,0:T(8,128)(2,1)} %get-tuple-element.20.grad, f32[2,16,1152]{2,1,0:T(8,128)} %get-tuple-element.21.sums), custom_call_target="tpu_custom_call" | custom-call | tf_op jit(solution)/shard_map/pallas_call | solution.py:619

commit v5 on v4

--- a/solution.py
+++ b/solution.py
@@ -307,14 +307,15 @@
     grad_out, sums_out,
     w, wo, so, order, hat, tqkv, back, tmixed, probs, dqkv, usend, urecv, up,
     tasend, tarecv, tmsend, tmrecv, asend, arecv, mrecv,
-    qkv, bsend, brecv, gpart, grecv, hsend, hrecv,
+    qkv, bsend, brecv, gpart, grecv, xsend, xrecv, hsend, hrecv,
     qbuf, kbuf, vbuf, bbuf, kt, pbuf, sbuf, dq, dk, dv, rsend, rrecv,
-    wsem, tosem, sosem, ordsem, qsem, uss, urs, mss, mrs, bss, brs, gss, grs, hss, hrs, rss, rrs,
+    wsem, tosem, sosem, ordsem, qsem, uss, urs, mss, mrs, bss, brs, gss, grs, xss, xrs, hss, hrs, rss, rrs,
 ):
     p = lax.axis_index("pos")
     f = lax.axis_index("frame")
     par = lax.rem(p, 2)
     chip = p // 2
+    y, half = lax.rem(f, 4), f // 4
     mate = p + 1 - 2 * par
     barrier = pltpu.get_barrier_semaphore()
     greet(barrier, p, f, True, True)
@@ -403,9 +404,11 @@
         c.start()
 
     def g_copy(g, s):
-        to = lax.rem(f + s, NF)
-        rows = pl.ds(pl.multiple_of(to * GS, 16), GS)
-        return send(gpart.at[g, rows], grecv.at[g, f], gss.at[g, s], grs.at[g, s], "frame", to)
+        to = lax.rem(y + s, 4)
+        rows = pl.ds(pl.multiple_of(to * 2 * GS, 16), 2 * GS)
+        return send(
+            gpart.at[g, rows], grecv.at[g, y], gss.at[g, s], grs.at[g, s], "frame", 4 * half + to
+        )
 
     def gradient(g, mine, left, theirs, right):
         for r in range(0, GH, 128):
@@ -413,11 +416,11 @@
             part += dot(theirs[:, r : r + 128], right[...], 0, 0)
             gpart[g, r : r + 128] = part.astype(BF)
 
-        @pl.loop(1, NF)
+        @pl.loop(1, 4)
         def _(s):
             g_copy(g, s).start()
 
-        grecv[g, pl.ds(f, 1)] = gpart[g, pl.ds(pl.multiple_of(f * GS, 16), GS)][None]
+        grecv[g, pl.ds(y, 1)] = gpart[g, pl.ds(pl.multiple_of(y * 2 * GS, 16), 2 * GS)][None]
 
     ta_copy.wait()
     tm_copy.wait()
@@ -474,6 +477,21 @@
         return send(
             hsend.at[g, to], hrecv.at[g, chip], hss.at[g, s], hrs.at[g, s], "pos", 2 * to + par
         )
+
+    def x_copy(g):
+        to = 4 * (1 - half) + y
+        return send(xsend.at[g, 1 - half], xrecv.at[g], xss.at[g], xrs.at[g], "frame", to)
+
+    def fold(g):
+        @pl.loop(1, 4)
+        def _(s):
+            g_copy(g, s).wait_recv()
+
+        total = grecv[g, 0].astype(F32)
+        for s in range(1, 4):
+            total += grecv[g, s].astype(F32)
+        xsend[g] = total.astype(BF).reshape(2, GS, D)
+        x_copy(g).start()
 
     for fr in range(FR):
         dk[...] = jnp.zeros_like(dk)
@@ -513,15 +531,12 @@
             r_copy(fr, s).start()
 
         rrecv[fr, pl.ds(p, 1)] = rsend[fr, pl.ds(p, 1)]
+        if fr == 0:
+            fold(0)
 
     def spread_out(g):
-        @pl.loop(1, NF)
-        def _(s):
-            g_copy(g, s).wait_recv()
-
-        total = grecv[g, 0].astype(F32)
-        for s in range(1, NF):
-            total += grecv[g, s].astype(F32)
+        x_copy(g).wait_recv()
+        total = xsend[g, half].astype(F32) + xrecv[g].astype(F32)
         hsend[g] = dot(spread[...], total.astype(BF), 1, 0).astype(BF).reshape(NK, 16, D)
 
         @pl.loop(1, NK)
@@ -548,6 +563,7 @@
     for c in w_copies:
         c.wait()
     finish_rows(0)
+    fold(1)
     spread_out(1)
     finish_rows(1)
     for g in range(2):
@@ -570,8 +586,14 @@
     @pl.loop(1, NF)
     def _(s):
         u_copy(s).wait_send()
+
+    @pl.loop(1, 4)
+    def _(s):
         for g in range(2):
             g_copy(g, s).wait_send()
+
+    for g in range(2):
+        x_copy(g).wait_send()
 
     @pl.loop(1, NK)
     def _(s):
@@ -594,15 +616,16 @@
             V((2, TT, GH), BF), V((TT, GH), BF), V((TT, D), BF), V((TT, D), BF),
             V((2, TOK, GH), BF), V((TOK, GH), BF), V((TOK, D), BF),
             V((FR, NP, PL, 256), BF), V((FR, NP, GRP, 256), BF), V((FR, NP, GRP, 256), BF),
-            V((2, GH, D), BF), V((2, NF, GS, D), BF), V((2, NK, 16, D), BF), V((2, NK, 16, D), BF),
+            V((2, GH, D), BF), V((2, 4, 2 * GS, D), BF),
+            V((2, 2, GS, D), BF), V((2, GS, D), BF), V((2, NK, 16, D), BF), V((2, NK, 16, D), BF),
             V((FR, ALL, 128), BF), V((FR, ALL, 128), BF), V((FR, ALL, 128), BF),
             V((NP, PL, 128), BF), V((FR, 128, ALL), BF),
             V((ALL, BT), BF), V((ALL, BT), BF),
             V((ALL, 128), F32), V((ALL, 128), F32), V((ALL, 128), F32),
             V((FR, NP, PL, 256), BF), V((FR, NP, PL, 256), BF),
             DMA((3,)), DMA, DMA, DMA, DMA, DMA((NF,)), DMA((NF,)), DMA((4,)), DMA((4,)),
-            DMA((FR, NP)), DMA((FR, NP)), DMA((2, NF)), DMA((2, NF)),
-            DMA((2, NK)), DMA((2, NK)), DMA((FR, NP)), DMA((FR, NP)),
+            DMA((FR, NP)), DMA((FR, NP)), DMA((2, 4)), DMA((2, 4)),
+            DMA((2,)), DMA((2,)), DMA((2, NK)), DMA((2, NK)), DMA((FR, NP)), DMA((FR, NP)),
         ],
         compiler_params=params(2),
     )(stream, cot, mask, unperm, spread, x, mixed, stat, att, order, tw, wo, qkv, w, so)
@@ -636,7 +659,8 @@
     spread = (row % 16 < GR)[:, None] & (((row // 16) * GR + row % 16)[:, None] == np.arange(GS)[None])
     col = np.arange(2 * GH)
     core, slab, inner = col // GH, col % GH // GS, col % GS
-    source = (slab * NP + 2 * (inner // GR) + core) * GR + inner % GR
+    frame = slab % 2 * 4 + slab // 2
+    source = (frame * NP + 2 * (inner // GR) + core) * GR + inner % GR
     order = (inner < NK * GR)[None] & (np.arange(D)[:, None] == source[None])
     order = order.reshape(D, 2, GH).transpose(1, 0, 2)
     return [jnp.asarray(t.astype(np.float32), BF) for t in (perm, perm.T, spread, order)] + [

time: 159 us -> 149 us (0.937)
  the two profiles are of different devices: /device:TPU:24 before, /device:TPU:1 now
where the time goes in v5:
time: 149 us
  Pallas kernels  149 us (100%)
    pallas_call x1, Pallas kernels, rest(): pl.pallas_call(rest_kernel, out_shape=(sds((TOK, D), BF), sds((2, 16, D),...  91.1 us
    pallas_call x1, Pallas kernels, space_forward(): pl.pallas_call(space_forward_kernel, out_shape=(sds((FR, NP, PL, 256), BF...  55.6 us

profile of v5, /device:TPU:1, one launch (start us, length us, event | category | flops | bytes accessed | tf_op | source)
XLA Modules:
  0.0 149.2 jit_solution(17374587416495554693)
XLA Ops:
  0.6 55.6 %shard_map.130 = (bf16[2,16,96,256]{3,2,1,0:T(8,128)(2,1)}, f32[2,8,1536]{2,1,0:T(8,128)}, f32[2,128,1536]{2,1,0:T(8,128)}, bf16[192,1152]{1,0:T(8,128)(2,1)}, b...) custom-call(bf16[192,1152]{1,0:T(8,128)(2,1)} %bitcast.5, bf16[192,1152]{1,0:T(8,128)(2,1)} %bitcast.9, ...), custom_call_target="tpu_custom_call" | custom-call | tf_op jit(solution)/shard_map/pallas_call | solution.py:279
  56.2 91.1 %shard_map.131 = (bf16[192,1152]{1,0:T(8,128)(2,1)}, f32[2,16,1152]{2,1,0:T(8,128)}) custom-call(bf16[256,1152]{1,0:T(8,128)(2,1)} %bitcast.7, bf16[256,1152]{1,0:T(8,128)(2,1)} %bitcast.8, f32[256,256]{1,0:T(8,128)} %constant.14.clone.mask, bf16[192,256]{1,0:T(8,128)(2,1)} %constant.11.clone.unperm, bf16[128,80]{1,0:T(8,128)(2,1)} %constant.12.clone.spread, ...), custom_call_target="tpu_custom_call" | custom-call | tf_op jit(solution)/shard_map/pallas_call | solution.py:607
  147.4 1.9 %shard_map.132 = (bf16[192,1152]{1,0:T(8,128)(2,1)}, f32[9,1152]{1,0:T(8,128)}, f32[9,1152]{1,0:T(8,128)}) custom-call(bf16[192,1152]{1,0:T(8,128)(2,1)} %get-tuple-element.20.grad, f32[2,16,1152]{2,1,0:T(8,128)} %get-tuple-element.21.sums), custom_call_target="tpu_custom_call" | custom-call | tf_op jit(solution)/shard_map/pallas_call | solution.py:642

commit v6 on v5

--- a/solution.py
+++ b/solution.py
@@ -307,18 +307,25 @@
     grad_out, sums_out,
     w, wo, so, order, hat, tqkv, back, tmixed, probs, dqkv, usend, urecv, up,
     tasend, tarecv, tmsend, tmrecv, asend, arecv, mrecv,
-    qkv, bsend, brecv, gpart, grecv, xsend, xrecv, hsend, hrecv,
+    qkv, bsend, brecv, gpart, grecv, hsend, hrecv,
     qbuf, kbuf, vbuf, bbuf, kt, pbuf, sbuf, dq, dk, dv, rsend, rrecv,
-    wsem, tosem, sosem, ordsem, qsem, uss, urs, mss, mrs, bss, brs, gss, grs, xss, xrs, hss, hrs, rss, rrs,
+    wsem, tosem, sosem, ordsem, qsem, uss, urs, mss, mrs, bss, brs, gss, grs, hss, hrs, rss, rrs,
 ):
     p = lax.axis_index("pos")
     f = lax.axis_index("frame")
     par = lax.rem(p, 2)
     chip = p // 2
     y, half = lax.rem(f, 4), f // 4
+    place = NK * half + chip
     mate = p + 1 - 2 * par
     barrier = pltpu.get_barrier_semaphore()
     greet(barrier, p, f, True, True)
+
+    @pl.loop(1, NK)
+    def _(s):
+        other = {"frame": 4 * (1 - half) + y, "pos": 2 * lax.rem(chip + s, NK) + par}
+        pl.semaphore_signal(barrier, inc=1, device_id=other)
+
     to_copy = pltpu.make_async_copy(to_hbm, wo, tosem)
     to_copy.start()
     tw_copies = [
@@ -363,7 +370,7 @@
         probs[h] = prob
         tmixed[:, win] += dot(prob.astype(BF), tqkv[2, :, win] * keep, 1, 0)
     tmsend[...] = tmixed[...].astype(BF)
-    pl.semaphore_wait(barrier, NP - 1 + NF - 1)
+    pl.semaphore_wait(barrier, NP - 1 + NF - 1 + NK - 1)
     ta_copy = send(tasend.at[1 - par], tarecv, mss.at[0], mrs.at[0], "pos", mate)
     tm_copy = send(tmsend, tmrecv, mss.at[1], mrs.at[1], "pos", mate)
     m_copy = send(mixed, mrecv, mss.at[2], mrs.at[2], "pos", mate)
@@ -473,14 +480,14 @@
         return send(rsend.at[fr, to], rrecv.at[fr, p], rss.at[fr, s], rrs.at[fr, s], "pos", to)
 
     def h_copy(g, s):
-        to = lax.rem(chip + s, NK)
-        return send(
-            hsend.at[g, to], hrecv.at[g, chip], hss.at[g, s], hrs.at[g, s], "pos", 2 * to + par
+        to = lax.rem(place + s, NP)
+        return pltpu.make_async_remote_copy(
+            src_ref=hsend.at[g, to],
+            dst_ref=hrecv.at[g, place],
+            send_sem=hss.at[g, s],
+            recv_sem=hrs.at[g, s],
+            device_id={"frame": 4 * (to // NK) + y, "pos": 2 * lax.rem(to, NK) + par},
         )
-
-    def x_copy(g):
-        to = 4 * (1 - half) + y
-        return send(xsend.at[g, 1 - half], xrecv.at[g], xss.at[g], xrs.at[g], "frame", to)
 
     def fold(g):
         @pl.loop(1, 4)
@@ -490,8 +497,13 @@
         total = grecv[g, 0].astype(F32)
         for s in range(1, 4):
             total += grecv[g, s].astype(F32)
-        xsend[g] = total.astype(BF).reshape(2, GS, D)
-        x_copy(g).start()
+        hsend[g] = dot(spread[...], total.astype(BF), 1, 0).astype(BF).reshape(NP, 16, D)
+
+        @pl.loop(1, NP)
+        def _(s):
+            h_copy(g, s).start()
+
+        hrecv[g, pl.ds(place, 1)] = hsend[g, pl.ds(place, 1)]
 
     for fr in range(FR):
         dk[...] = jnp.zeros_like(dk)
@@ -534,17 +546,6 @@
         if fr == 0:
             fold(0)
 
-    def spread_out(g):
-        x_copy(g).wait_recv()
-        total = xsend[g, half].astype(F32) + xrecv[g].astype(F32)
-        hsend[g] = dot(spread[...], total.astype(BF), 1, 0).astype(BF).reshape(NK, 16, D)
-
-        @pl.loop(1, NK)
-        def _(s):
-            h_copy(g, s).start()
-
-        hrecv[g, pl.ds(chip, 1)] = hsend[g, pl.ds(chip, 1)]
-
     def finish_rows(fr):
         @pl.loop(1, NP)
         def _(s):
@@ -559,21 +560,19 @@
         normed, inv = normalize(x[here])
         grad_out[here] = (up[here].astype(F32) + norm_back(grad_hat, normed, inv)).astype(BF)
 
-    spread_out(0)
     for c in w_copies:
         c.wait()
     finish_rows(0)
     fold(1)
-    spread_out(1)
     finish_rows(1)
     for g in range(2):
 
-        @pl.loop(1, NK)
+        @pl.loop(1, NP)
         def _(s):
             h_copy(g, s).wait_recv()
 
         total = hrecv[g, 0].astype(F32)
-        for s in range(1, NK):
+        for s in range(1, NP):
             total += hrecv[g, s].astype(F32)
         sums_out[g] = total
 
@@ -582,6 +581,8 @@
         for fr in range(FR):
             b_copy(fr, s).wait_send()
             r_copy(fr, s).wait_send()
+        for g in range(2):
+            h_copy(g, s).wait_send()
 
     @pl.loop(1, NF)
     def _(s):
@@ -591,14 +592,6 @@
     def _(s):
         for g in range(2):
             g_copy(g, s).wait_send()
-
-    for g in range(2):
-        x_copy(g).wait_send()
-
-    @pl.loop(1, NK)
-    def _(s):
-        for g in range(2):
-            h_copy(g, s).wait_send()
 
 
 def rest(stream, cot, mask, unperm, spread, x, mixed, stat, att, order, tw, wo, qkv, w, so):
@@ -617,7 +610,7 @@
             V((2, TOK, GH), BF), V((TOK, GH), BF), V((TOK, D), BF),
             V((FR, NP, PL, 256), BF), V((FR, NP, GRP, 256), BF), V((FR, NP, GRP, 256), BF),
             V((2, GH, D), BF), V((2, 4, 2 * GS, D), BF),
-            V((2, 2, GS, D), BF), V((2, GS, D), BF), V((2, NK, 16, D), BF), V((2, NK, 16, D), BF),
+            V((2, NP, 16, D), BF), V((2, NP, 16, D), BF),
             V((FR, ALL, 128), BF), V((FR, ALL, 128), BF), V((FR, ALL, 128), BF),
             V((NP, PL, 128), BF), V((FR, 128, ALL), BF),
             V((ALL, BT), BF), V((ALL, BT), BF),
@@ -625,7 +618,7 @@
             V((FR, NP, PL, 256), BF), V((FR, NP, PL, 256), BF),
             DMA((3,)), DMA, DMA, DMA, DMA, DMA((NF,)), DMA((NF,)), DMA((4,)), DMA((4,)),
             DMA((FR, NP)), DMA((FR, NP)), DMA((2, 4)), DMA((2, 4)),
-            DMA((2,)), DMA((2,)), DMA((2, NK)), DMA((2, NK)), DMA((FR, NP)), DMA((FR, NP)),
+            DMA((2, NP)), DMA((2, NP)), DMA((FR, NP)), DMA((FR, NP)),
         ],
         compiler_params=params(2),
     )(stream, cot, mask, unperm, spread, x, mixed, stat, att, order, tw, wo, qkv, w, so)
@@ -655,8 +648,9 @@
     perm = (real[:, None] & (col[:, None] == np.arange(TOK)[None])).astype(np.float32)
     place = np.where(real, inner % TP, -1)
     mask = np.where(place[:, None] == place[None], 0.0, -1e30).astype(np.float32)
-    row = np.arange(NK * 16)
-    spread = (row % 16 < GR)[:, None] & (((row // 16) * GR + row % 16)[:, None] == np.arange(GS)[None])
+    row = np.arange(NP * 16)
+    source = row // 16 // NK * GS + row // 16 % NK * GR + row % 16
+    spread = (row % 16 < GR)[:, None] & (source[:, None] == np.arange(2 * GS)[None])
     col = np.arange(2 * GH)
     core, slab, inner = col // GH, col % GH // GS, col % GS
     frame = slab % 2 * 4 + slab // 2

time: 149 us -> 149 us (level)
  no operation moved by 1% of the time
where the time goes in v6:
time: 149 us; the launch traced here: 148 us
  Pallas kernels  148 us (99%)
    pallas_call x1, Pallas kernels, rest(): pl.pallas_call(rest_kernel, out_shape=(sds((TOK, D), BF), sds((2, 16, D),...  90.4 us
    pallas_call x1, Pallas kernels, space_forward(): pl.pallas_call(space_forward_kernel, out_shape=(sds((FR, NP, PL, 256), BF...  55.6 us

profile of v6, /device:TPU:1, one launch (start us, length us, event | category | flops | bytes accessed | tf_op | source)
XLA Modules:
  0.0 148.4 jit_solution(6257554669492217641)
XLA Ops:
  0.6 55.6 %shard_map.130 = (bf16[2,16,96,256]{3,2,1,0:T(8,128)(2,1)}, f32[2,8,1536]{2,1,0:T(8,128)}, f32[2,128,1536]{2,1,0:T(8,128)}, bf16[192,1152]{1,0:T(8,128)(2,1)}, b...) custom-call(bf16[192,1152]{1,0:T(8,128)(2,1)} %bitcast.5, bf16[192,1152]{1,0:T(8,128)(2,1)} %bitcast.9, ...), custom_call_target="tpu_custom_call" | custom-call | tf_op jit(solution)/shard_map/pallas_call | solution.py:279
  56.2 90.4 %shard_map.131 = (bf16[192,1152]{1,0:T(8,128)(2,1)}, f32[2,16,1152]{2,1,0:T(8,128)}) custom-call(bf16[256,1152]{1,0:T(8,128)(2,1)} %bitcast.7, bf16[256,1152]{1,0:T(8,128)(2,1)} %bitcast.8, f32[256,256]{1,0:T(8,128)} %constant.14.clone.mask, bf16[192,256]{1,0:T(8,128)(2,1)} %constant.11.clone.unperm, bf16[256,160]{1,0:T(8,128)(2,1)} %constant.12.clone.spread, ...), custom_call_target="tpu_custom_call" | custom-call | tf_op jit(solution)/shard_map/pallas_call | solution.py:600
  146.6 1.9 %shard_map.132 = (bf16[192,1152]{1,0:T(8,128)(2,1)}, f32[9,1152]{1,0:T(8,128)}, f32[9,1152]{1,0:T(8,128)}) custom-call(bf16[192,1152]{1,0:T(8,128)(2,1)} %get-tuple-element.20.grad, f32[2,16,1152]{2,1,0:T(8,128)} %get-tuple-element.21.sums), custom_call_target="tpu_custom_call" | custom-call | tf_op jit(solution)/shard_map/pallas_call | solution.py:635

commit v7 on v6

--- a/solution.py
+++ b/solution.py
@@ -87,10 +87,10 @@
 
 
 def space_forward_kernel(
-    x, cot, perm, w_hbm, so_hbm,
-    qkv_out, stat_out, att_out, mixed_out, stream_out, cot_out,
-    w, so, hat, qsend, qkv, kbuf, qbuf, vt, sbuf, pbuf, osend, orecv, stream, fsend, frecv, csend, crecv,
-    wsem, sosem, qss, qrs, oss, ors, fss, frs, css, crs, outsem,
+    x, cot, perm, w_hbm, so_hbm, wo_hbm, order_hbm,
+    qkv_out, stat_out, att_out, mixed_out, stream_out, cot_out, back_out, split_out,
+    w, so, wo, order, hat, qsend, qkv, kbuf, qbuf, vt, sbuf, pbuf, osend, orecv, stream, fsend, frecv, csend, crecv,
+    wsem, sosem, wosem, ordsem, qss, qrs, oss, ors, fss, frs, css, crs, outsem,
 ):
     p = lax.axis_index("pos")
     f = lax.axis_index("frame")
@@ -107,7 +107,8 @@
         for c in range(3):
             w_copy(i, c).start()
     so_copy = pltpu.make_async_copy(so_hbm, so, sosem)
-    so_copy.start()
+    wo_copy = pltpu.make_async_copy(wo_hbm, wo, wosem)
+    order_copy = pltpu.make_async_copy(order_hbm, order, ordsem)
     hat[...] = normalize(x[...])[0].astype(BF)
     pl.semaphore_wait(barrier, NP - 1 + NF - 1)
 
@@ -136,6 +137,8 @@
         q_copy(1, s).start()
 
     qkv[:, pl.ds(p, 1)] = qsend[0][:, None]
+    for late in (so_copy, wo_copy, order_copy):
+        late.start()
 
     def c_copy(s):
         to = lax.rem(f + s, NF)
@@ -234,6 +237,12 @@
         c_copy(s).wait_recv()
 
     cot_out[...] = crecv[...]
+    tcot = crecv[...].reshape(TT, D)
+    wo_copy.wait()
+    back_out[...] = dot(tcot, wo[...], 1, 0).astype(BF)
+    order_copy.wait()
+    for e in range(2):
+        split_out[e] = dot(tcot, order[e], 1, 0).astype(BF)
 
     @pl.loop(1, NP)
     def _(s):
@@ -273,7 +282,7 @@
     )
 
 
-def space_forward(x, cot, perm, w, so):
+def space_forward(x, cot, perm, w, so, wo, order):
     V = pltpu.VMEM
     sds = jax.ShapeDtypeStruct
     return pl.pallas_call(
@@ -285,31 +294,33 @@
             sds((TOK, D), BF),
             sds((NF, SLAB, D), BF),
             sds((NF, SLAB, D), BF),
+            sds((TT, D), BF),
+            sds((2, TT, GH), BF),
         ),
-        in_specs=[vmem(), vmem(), vmem(), anywhere(), anywhere()],
-        out_specs=(anywhere(), vmem(), vmem(), vmem(), vmem(), vmem()),
+        in_specs=[vmem(), vmem(), vmem()] + [anywhere()] * 4,
+        out_specs=(anywhere(),) + (vmem(),) * 7,
         scratch_shapes=[
-            V((8, 432, D), BF), V((D, D), BF), V((TOK, D), BF), V((NP, FR, PL, 256), BF),
+            V((8, 432, D), BF), V((D, D), BF), V((D, D), BF), V((2, D, GH), BF), V((TOK, D), BF), V((NP, FR, PL, 256), BF),
             V((FR, NP, PL, 256), BF), V((ALL, 128), BF), V((ALL, 128), BF), V((128, ALL), BF),
             V((ALL, QT), F32), V((ALL, QT), BF),
             V((FR, NP, GRP, 256), BF), V((FR, NP, GRP, 256), BF), V((TOK, D), BF),
             V((NF, SLAB, D), BF), V((NF, SLAB, D), BF), V((NF, SLAB, D), BF), V((NF, SLAB, D), BF),
-            DMA((8, 3)), DMA, DMA((FR, NP)), DMA((FR, NP)), DMA((FR, NP)), DMA((FR, NP)),
+            DMA((8, 3)), DMA, DMA, DMA, DMA((FR, NP)), DMA((FR, NP)), DMA((FR, NP)), DMA((FR, NP)),
             DMA((NF,)), DMA((NF,)), DMA((NF,)), DMA((NF,)), DMA((FR,)),
         ],
         compiler_params=params(1),
-    )(x, cot, perm, w, so)
+    )(x, cot, perm, w, so, wo, order)
 
 
 def rest_kernel(
-    stream, cot, mask, unperm, spread, x, mixed, stat, att,
-    order_hbm, tw_hbm, to_hbm, qkv_hbm, w_hbm, so_hbm,
+    stream, cot, back, tasend, mask, unperm, spread, x, mixed, stat, att,
+    order_hbm, tw_hbm, qkv_hbm, w_hbm, so_hbm,
     grad_out, sums_out,
-    w, wo, so, order, hat, tqkv, back, tmixed, probs, dqkv, usend, urecv, up,
-    tasend, tarecv, tmsend, tmrecv, asend, arecv, mrecv,
+    w, so, order, hat, tqkv, tmixed, probs, dqkv, usend, urecv, up,
+    tarecv, tmsend, tmrecv, asend, arecv, mrecv,
     qkv, bsend, brecv, gpart, grecv, hsend, hrecv,
     qbuf, kbuf, vbuf, bbuf, kt, pbuf, sbuf, dq, dk, dv, rsend, rrecv,
-    wsem, tosem, sosem, ordsem, qsem, uss, urs, mss, mrs, bss, brs, gss, grs, hss, hrs, rss, rrs,
+    wsem, sosem, ordsem, qsem, uss, urs, mss, mrs, bss, brs, gss, grs, hss, hrs, rss, rrs,
 ):
     p = lax.axis_index("pos")
     f = lax.axis_index("frame")
@@ -326,31 +337,23 @@
         other = {"frame": 4 * (1 - half) + y, "pos": 2 * lax.rem(chip + s, NK) + par}
         pl.semaphore_signal(barrier, inc=1, device_id=other)
 
-    to_copy = pltpu.make_async_copy(to_hbm, wo, tosem)
-    to_copy.start()
     tw_copies = [
         pltpu.make_async_copy(tw_hbm.at[pl.ds(c * D, D)], w.at[c], wsem.at[c]) for c in range(3)
     ]
     for c in tw_copies:
         c.start()
     order_copy = pltpu.make_async_copy(order_hbm, order, ordsem)
-    order_copy.start()
     so_copy = pltpu.make_async_copy(so_hbm, so, sosem)
-    so_copy.start()
     qkv_copy = pltpu.make_async_copy(qkv_hbm, qkv, qsem)
-    qkv_copy.start()
 
     normed, inv = normalize(stream[...])
     hat[...] = normed
     normed = normed.astype(BF)
-    to_copy.wait()
-    back[...] = dot(cot[...], wo[...], 1, 0).astype(BF)
     for c in range(3):
         tw_copies[c].wait()
         tqkv[c] = dot(normed, w[c], 1, 1).astype(BF)
-    order_copy.wait()
-    for e in range(2):
-        tasend[e] = dot(cot[...], order[e], 1, 0).astype(BF)
+    for late in (qkv_copy, so_copy, order_copy):
+        late.start()
     tmixed[...] = jnp.zeros_like(tmixed)
     dqkv[...] = jnp.zeros_like(dqkv)
 
@@ -467,6 +470,7 @@
             b_copy(fr, s).start()
 
     brecv[:, pl.ds(p, 1)] = bsend[:, pl.ds(p, 1)]
+    order_copy.wait()
     for e in range(2):
         asend[e] = dot(up[...], order[e], 1, 0).astype(BF)
     a_copy = send(asend.at[1 - par], arecv, mss.at[3], mrs.at[3], "pos", mate)
@@ -594,19 +598,19 @@
             g_copy(g, s).wait_send()
 
 
-def rest(stream, cot, mask, unperm, spread, x, mixed, stat, att, order, tw, wo, qkv, w, so):
+def rest(stream, cot, back, split, mask, unperm, spread, x, mixed, stat, att, order, tw, qkv, w, so):
     V = pltpu.VMEM
     sds = jax.ShapeDtypeStruct
     return pl.pallas_call(
         rest_kernel,
         out_shape=(sds((TOK, D), BF), sds((2, 16, D), F32)),
-        in_specs=[vmem()] * 9 + [anywhere()] * 6,
+        in_specs=[vmem()] * 11 + [anywhere()] * 5,
         out_specs=(vmem(), vmem()),
         scratch_shapes=[
-            V((3, D, D), BF), V((D, D), BF), V((D, D), BF), V((2, D, GH), BF), V((TT, D), F32),
-            V((3, TT, D), BF), V((TT, D), BF), V((TT, D), F32), V((HEADS, TT, TT), F32),
+            V((3, D, D), BF), V((D, D), BF), V((2, D, GH), BF), V((TT, D), F32),
+            V((3, TT, D), BF), V((TT, D), F32), V((HEADS, TT, TT), F32),
             V((3, TT, D), F32), V((NF, SLAB, D), BF), V((NF, SLAB, D), BF), V((TOK, D), BF),
-            V((2, TT, GH), BF), V((TT, GH), BF), V((TT, D), BF), V((TT, D), BF),
+            V((TT, GH), BF), V((TT, D), BF), V((TT, D), BF),
             V((2, TOK, GH), BF), V((TOK, GH), BF), V((TOK, D), BF),
             V((FR, NP, PL, 256), BF), V((FR, NP, GRP, 256), BF), V((FR, NP, GRP, 256), BF),
             V((2, GH, D), BF), V((2, 4, 2 * GS, D), BF),
@@ -616,12 +620,12 @@
             V((ALL, BT), BF), V((ALL, BT), BF),
             V((ALL, 128), F32), V((ALL, 128), F32), V((ALL, 128), F32),
             V((FR, NP, PL, 256), BF), V((FR, NP, PL, 256), BF),
-            DMA((3,)), DMA, DMA, DMA, DMA, DMA((NF,)), DMA((NF,)), DMA((4,)), DMA((4,)),
+            DMA((3,)), DMA, DMA, DMA, DMA((NF,)), DMA((NF,)), DMA((4,)), DMA((4,)),
             DMA((FR, NP)), DMA((FR, NP)), DMA((2, 4)), DMA((2, 4)),
             DMA((2, NP)), DMA((2, NP)), DMA((FR, NP)), DMA((FR, NP)),
         ],
         compiler_params=params(2),
-    )(stream, cot, mask, unperm, spread, x, mixed, stat, att, order, tw, wo, qkv, w, so)
+    )(stream, cot, back, split, mask, unperm, spread, x, mixed, stat, att, order, tw, qkv, w, so)
 
 
 def finish_kernel(grad, sums, grad_out, gs_out, gt_out):
@@ -666,10 +670,12 @@
     perm, unperm, spread, order, mask = tables()
     x = inputs.reshape(TOK, D)
     cot = cotangent.reshape(TOK, D)
-    qkv, stat, att, mixed, stream_t, cot_t = space_forward(x, cot, perm, space_projection, space_output)
+    qkv, stat, att, mixed, stream_t, cot_t, back, split = space_forward(
+        x, cot, perm, space_projection, space_output, time_output, order
+    )
     grad, sums = rest(
-        stream_t.reshape(TT, D), cot_t.reshape(TT, D), mask, unperm, spread, x, mixed, stat, att,
-        order, time_projection, time_output, qkv, space_projection, space_output,
+        stream_t.reshape(TT, D), cot_t.reshape(TT, D), back, split, mask, unperm, spread, x, mixed,
+        stat, att, order, time_projection, qkv, space_projection, space_output,
     )
     grad, gs, gt = finish(grad, sums)
     return grad.reshape(FR, PL, D), gs, gt

time: 149 us -> 145 us (0.973)
  Pallas kernels: 148 us -> 144 us
    pallas_call x1, Pallas kernels: 90.4 us -> 86.6 us  [rest(): pl.pallas_call(rest_kernel, out_shape=(sds((TOK, D), BF), sds((2, 16, D),...]
where the time goes in v7:
time: 145 us
  Pallas kernels  144 us (99%)
    pallas_call x1, Pallas kernels, rest(): pl.pallas_call(rest_kernel, out_shape=(sds((TOK, D), BF), sds((2, 16, D),...  86.6 us
    pallas_call x1, Pallas kernels, space_forward(): pl.pallas_call(space_forward_kernel, out_shape=(sds((FR, NP, PL, 256), BF...  56 us

profile of v7, /device:TPU:1, one launch (start us, length us, event | category | flops | bytes accessed | tf_op | source)
XLA Modules:
  0.0 145.1 jit_solution(14968845927796550424)
XLA Ops:
  0.6 56.0 %shard_map.130 = (bf16[2,16,96,256]{3,2,1,0:T(8,128)(2,1)}, f32[2,8,1536]{2,1,0:T(8,128)}, f32[2,128,1536]{2,1,0:T(8,128)}, bf16[192,1152]{1,0:T(8,128)(2,1)}, b...) custom-call(bf16[192,1152]{1,0:T(8,128)(2,1)} %bitcast.5, ...), custom_call_target="tpu_custom_call" | custom-call | tf_op jit(solution)/shard_map/pallas_call | solution.py:288
  56.6 86.6 %shard_map.131 = (bf16[192,1152]{1,0:T(8,128)(2,1)}, f32[2,16,1152]{2,1,0:T(8,128)}) custom-call(bf16[256,1152]{1,0:T(8,128)(2,1)} %bitcast.7, bf16[256,1152]{1,0:T(8,128)(2,1)} %bitcast.8, bf16[256,1152]{1,0:T(8,128)(2,1)} %get-tuple-element.18.back, bf16[2,256,640]{2,1,0:T(8,128)(2,1)} %get-tuple-element.19.tasend, f32[256,256]{1,0:T(8,128)} %constant.14.clone.mask, ...), custom_call_target="tpu_custom_call" | custom-call | tf_op jit(solution)/shard_map/pallas_call | solution.py:604
  143.2 1.9 %shard_map.132 = (bf16[192,1152]{1,0:T(8,128)(2,1)}, f32[9,1152]{1,0:T(8,128)}, f32[9,1152]{1,0:T(8,128)}) custom-call(bf16[192,1152]{1,0:T(8,128)(2,1)} %get-tuple-element.24.grad, f32[2,16,1152]{2,1,0:T(8,128)} %get-tuple-element.25.sums), custom_call_target="tpu_custom_call" | custom-call | tf_op jit(solution)/shard_map/pallas_call | solution.py:639

commit v8 on v7

--- a/solution.py
+++ b/solution.py
@@ -176,7 +176,7 @@
 
         @pl.loop(0, ALL // QT)
         def _(t):
-            tile = lax.rem(p // 4 + t, ALL // QT)
+            tile = lax.rem(p // 4 + ALL // QT - 1 - t, ALL // QT)
             at = pl.ds(pl.multiple_of(tile * QT, QT), QT)
             q = qbuf[at]
             top = jnp.full((8, QT), -jnp.inf, F32)
@@ -193,7 +193,7 @@
             total = jnp.sum(total, axis=0, keepdims=True)
             o = dot(vt[...], pbuf[...], 1, 0) * (1.0 / total)
             stat_out[fr, :, at] = jnp.broadcast_to(top + jnp.log(total) * LOG2E, (8, QT))
-            att_out[fr, :, at] = o
+            att_out[fr, :, at] = o[:HD]
             turned = o.T.reshape(4, 3, GRP, 128)
             osend[fr, pl.ds(tile * 4, 4)] = pack([turned[:, g, :, :HD] for g in range(3)])
             for j in range(4):
@@ -290,7 +290,7 @@
         out_shape=(
             sds((FR, NP, PL, 256), BF),
             sds((FR, 8, ALL), F32),
-            sds((FR, 128, ALL), F32),
+            sds((FR, HD, ALL), F32),
             sds((TOK, D), BF),
             sds((NF, SLAB, D), BF),
             sds((NF, SLAB, D), BF),
@@ -527,7 +527,7 @@
             at = pl.ds(pl.multiple_of(t * BT, BT), BT)
             q = qbuf[fr, at]
             b = bbuf.reshape(ALL, 128)[at]
-            total = jnp.sum(b.astype(F32).T * att[fr, :, at], axis=0, keepdims=True)
+            total = jnp.sum(b.astype(F32).T[:HD] * att[fr, :, at], axis=0, keepdims=True)
             lse = stat[fr, 0:1, at]
             for k in range(0, ALL, KC):
                 s = dot(kbuf[fr, k : k + KC], q, 1, 1)

time: 145 us -> 143 us (0.986)
  Pallas kernels: 144 us -> 141 us
    pallas_call x1, Pallas kernels: 86.6 us -> 82.4 us  [rest(): pl.pallas_call(rest_kernel, out_shape=(sds((TOK, D), BF), sds((2, 16, D),...]
where the time goes in v8:
time: 143 us; the launch traced here: 142 us
  Pallas kernels  141 us (99%)
    pallas_call x1, Pallas kernels, rest(): pl.pallas_call(rest_kernel, out_shape=(sds((TOK, D), BF), sds((2, 16, D),...  82.4 us
    pallas_call x1, Pallas kernels, space_forward(): pl.pallas_call(space_forward_kernel, out_shape=(sds((FR, NP, PL, 256), BF...  57.1 us

profile of v8, /device:TPU:1, one launch (start us, length us, event | category | flops | bytes accessed | tf_op | source)
XLA Modules:
  0.0 142.0 jit_solution(9551160217643609005)
XLA Ops:
  0.6 57.1 %shard_map.130 = (bf16[2,16,96,256]{3,2,1,0:T(8,128)(2,1)}, f32[2,8,1536]{2,1,0:T(8,128)}, f32[2,72,1536]{2,1,0:T(8,128)}, bf16[192,1152]{1,0:T(8,128)(2,1)}, bf...) custom-call(bf16[192,1152]{1,0:T(8,128)(2,1)} %bitcast.5, ...), custom_call_target="tpu_custom_call" | custom-call | tf_op jit(solution)/shard_map/pallas_call | solution.py:288
  57.7 82.4 %shard_map.131 = (bf16[192,1152]{1,0:T(8,128)(2,1)}, f32[2,16,1152]{2,1,0:T(8,128)}) custom-call(bf16[256,1152]{1,0:T(8,128)(2,1)} %bitcast.7, bf16[256,1152]{1,0:T(8,128)(2,1)} %bitcast.8, bf16[256,1152]{1,0:T(8,128)(2,1)} %get-tuple-element.18.back, bf16[2,256,640]{2,1,0:T(8,128)(2,1)} %get-tuple-element.19.tasend, f32[256,256]{1,0:T(8,128)} %constant.14.clone.mask, ...), custom_call_target="tpu_custom_call" | custom-call | tf_op jit(solution)/shard_map/pallas_call | solution.py:604
  140.1 1.9 %shard_map.132 = (bf16[192,1152]{1,0:T(8,128)(2,1)}, f32[9,1152]{1,0:T(8,128)}, f32[9,1152]{1,0:T(8,128)}) custom-call(bf16[192,1152]{1,0:T(8,128)(2,1)} %get-tuple-element.24.grad, f32[2,16,1152]{2,1,0:T(8,128)} %get-tuple-element.25.sums), custom_call_target="tpu_custom_call" | custom-call | tf_op jit(solution)/shard_map/pallas_call | solution.py:639
